TPU v7x, 32 devices: a whole 2x2x4 slice. The times are simulated.
32 devices in a mesh: leaf: 8 (over z, x), batch: 4 (over y, core).
Axes of the slice: x: 2, y: 2, z: 4, core: 2. Of those that a mesh axis runs over, the one named last changes fastest.
Arguments:
- pixels_low: int32 [80, 512], P('leaf', 'batch'), may hold values from 0 to 255
- pixels_mid: int32 [32, 512], P('leaf', 'batch'), may hold values from 0 to 255
- pixels_top: int32 [8, 512], P('leaf', 'batch'), may hold values from 0 to 255
- emit_low: bfloat16 [80, 256, 256], P('leaf'), may hold values from -153 to 0, as said below
- emit_mid: bfloat16 [32, 256, 256], P('leaf'), may hold values from -153 to 0, as said below
- emit_top: bfloat16 [8, 256, 256], P('leaf'), may hold values from -153 to 0, as said below
- trans_low: bfloat16 [80, 256, 256], P('leaf'), may hold values from 0.0001171875 to 3.515625, as said below
- trans_mid: bfloat16 [32, 256, 256], P('leaf'), may hold values from 0.0001171875 to 3.515625, as said below
- outside_top: float32 [8, 512, 256], P('leaf', 'batch'), may hold values from -1708 to -292, as said below
- parent_low: int32 [80], replicated, may hold values from 0 to 31, as said below
- parent_mid: int32 [32], replicated, may hold values from 0 to 7
Outputs:
- update_low: float32 [80, 256, 256], P('leaf', 'batch')
- update_mid: float32 [32, 256, 256], P('leaf', 'batch')
Inputs may be any that keep to these rules, and one draw needn't show every extreme that they name: `emit_low`: Log-probabilities of pixel values given a state. `emit_mid`: Log-probabilities of pixel values given a state. `emit_top`: Log-probabilities of pixel values given a state. `trans_low`: positive edge weights. `trans_mid`: positive edge weights. `outside_top`: Log-likelihood of the rest of the image given a state. `parent_low`: among the 10 bottom-level nodes of one leaf index, at most 3 have a parent p held by another leaf index (leaf index p // 4); some leaf index has exactly 3.
All inputs are finite; a program needn't handle non-finite values.
Results may differ from a plain program's by a relative error of at most 0.0015.
Values sent between devices are 32-bit elements; how exact they have to be, the bound alone decides.
A program may use at most 64 MiB of HBM per device.

v0:
```python
import jax
import jax.numpy as jnp
from jax import lax
from jax.sharding import PartitionSpec as P

PSEUDO = 0.001


def lookup_all(table, pixels):
    levels = jnp.arange(table.shape[1], dtype=jnp.int32)
    picks = (pixels[:, :, None] == levels[None, None, :]).astype(jnp.bfloat16)
    return jnp.einsum("nbv,nvk->nbk", picks, table, preferred_element_type=jnp.float32)


def upward_all(inside, weight):
    top = jnp.max(inside, axis=-1, keepdims=True)
    scaled = jnp.exp(inside - top).astype(jnp.bfloat16)
    linear = jnp.einsum("nbj,nij->nbi", scaled, weight, preferred_element_type=jnp.float32)
    return (jnp.log(linear) + top, scaled)


def edge_all(above, weight, scaled):
    peak = jnp.max(above, axis=-1, keepdims=True)
    pushed = jnp.exp(above - peak).astype(jnp.bfloat16)
    reach = jnp.einsum("nbi,nij->nbj", pushed, weight, preferred_element_type=jnp.float32)
    total = jnp.sum(reach * scaled.astype(jnp.float32), axis=-1, keepdims=True)
    share = (pushed.astype(jnp.float32) / total).astype(jnp.bfloat16)
    counts = jnp.einsum("nbi,nbj->nij", share, scaled, preferred_element_type=jnp.float32)
    return (counts * weight.astype(jnp.float32), jnp.log(reach) + peak)


def finish(summed):
    counts = summed + PSEUDO
    return counts.shape[-1] * counts / jnp.sum(counts, axis=-1, keepdims=True)


def body(
    pixels_low,
    pixels_mid,
    pixels_top,
    emit_low,
    emit_mid,
    emit_top,
    trans_low,
    trans_mid,
    outside_top,
    parent_low,
    parent_mid,
):
    devices = lax.axis_size("leaf")
    mid_count = emit_mid.shape[0]
    top_count = emit_top.shape[0]
    up_low, scaled_low = upward_all(lookup_all(emit_low, pixels_low), trans_low)
    emis_mid = lookup_all(emit_mid, pixels_mid)
    emis_top = lookup_all(emit_top, pixels_top)
    moved = lax.all_to_all(up_low, "leaf", split_axis=1, concat_axis=0, tiled=True)
    gathered_mid = jax.ops.segment_sum(moved, parent_low, num_segments=mid_count * devices)
    sums_mid = lax.all_to_all(gathered_mid, "leaf", split_axis=0, concat_axis=1, tiled=True)
    inside_mid = emis_mid + sums_mid
    up_mid, scaled_mid = upward_all(inside_mid, trans_mid)
    moved_mid = lax.all_to_all(up_mid, "leaf", split_axis=1, concat_axis=0, tiled=True)
    gathered_top = jax.ops.segment_sum(moved_mid, parent_mid, num_segments=top_count * devices)
    sums_top = lax.all_to_all(gathered_top, "leaf", split_axis=0, concat_axis=1, tiled=True)
    total_top = emis_top + sums_top + outside_top
    spread_top = lax.all_to_all(total_top, "leaf", split_axis=1, concat_axis=0, tiled=True)
    picked = lax.all_to_all(spread_top[parent_mid], "leaf", split_axis=0, concat_axis=1, tiled=True)
    counts_mid, outside_mid = edge_all(picked - up_mid, trans_mid, scaled_mid)
    update_mid = finish(lax.psum_scatter(counts_mid, "batch", scatter_dimension=1, tiled=True))
    total_mid = inside_mid + outside_mid
    spread_mid = lax.all_to_all(total_mid, "leaf", split_axis=1, concat_axis=0, tiled=True)
    above_low = lax.all_to_all(
        spread_mid[parent_low], "leaf", split_axis=0, concat_axis=1, tiled=True
    )
    counts_low, unused = edge_all(above_low - up_low, trans_low, scaled_low)
    update_low = finish(lax.psum_scatter(counts_low, "batch", scatter_dimension=1, tiled=True))
    return (update_low, update_mid)


def solution(mesh):
    return jax.shard_map(
        body,
        mesh=mesh,
        in_specs=(
            P("leaf", "batch"),
            P("leaf", "batch"),
            P("leaf", "batch"),
            P("leaf", None, None),
            P("leaf", None, None),
            P("leaf", None, None),
            P("leaf", None, None),
            P("leaf", None, None),
            P("leaf", "batch", None),
            P(),
            P(),
        ),
        out_specs=(P("leaf", "batch", None), P("leaf", "batch", None)),
        check_vma=False,
    )
```

profile of v0, /device:TPU:0, one launch (start us, length us, event | category | flops | bytes accessed | tf_op | source)
XLA Modules:
  0.0 264.6 jit_solution(11058468682332525824)
XLA Ops:
  7.2 1.3 copy-done
  8.5 1.5 fusion.28
  10.0 1.1 copy-done.1
  11.1 0.8 fusion.2
  11.9 0.8 copy.32
  12.7 55.3 %all_to_all.132 = f32[10,128,256]{2,0,1:T(8,128)S(1)} all-to-all(f32[10,128,256]{2,0,1:T(8,128)S(1)} %copy.32), channel_id=1, replica_groups=mesh['leaf'=8,'batch'=4] {'leaf'}, dimensions={1} | all-to-all | bytes 2621440 | tf_op jit(solution)/shard_map/all_to_all | solution.py:56
  68.0 1.8 copy.34
  69.9 7.6 %scatter_fusion = f32[32,16,256]{2,1,0:T(8,128)S(1)} fusion(f32[32,16,256]{2,1,0:T(8,128)S(1)} %broadcast_in_dim.12, s32[80]{0:T(128)S(1)} %copy-done.13, f32[80,16,256]{2,1,0:T(8,128)} %bitcast.57), kind=kCustom, calls=%fused_computation.2 | custom fusion | flops 327680 | bytes 3932480 | tf_op jit(solution)/shard_map/scatter-add | solution.py:57
  77.5 17.7 %all_to_all.133 = f32[32,16,256]{2,1,0:T(8,128)S(1)} all-to-all(f32[32,16,256]{2,1,0:T(8,128)S(1)} %scatter_fusion), channel_id=1, replica_groups=mesh['leaf'=8,'batch'=4] {'leaf'}, dimensions={0} | all-to-all | bytes 1048576 | tf_op jit(solution)/shard_map/all_to_all | solution.py:58
  95.2 0.4 fusion.29
  95.6 0.6 copy-done.5
  96.2 0.3 fusion.6
  96.5 0.3 copy.36
  96.9 17.4 %all_to_all.134 = f32[4,128,256]{2,0,1:T(4,128)S(1)} all-to-all(f32[4,128,256]{2,0,1:T(4,128)S(1)} %copy.36), channel_id=1, replica_groups=mesh['leaf'=8,'batch'=4] {'leaf'}, dimensions={1} | all-to-all | bytes 1048576 | tf_op jit(solution)/shard_map/all_to_all | solution.py:61
  114.3 0.1 copy.37
  114.5 0.8 copy.38
  115.3 3.5 %scatter_fusion.1 = f32[8,16,256]{2,1,0:T(8,128)S(1)} fusion(f32[8,16,256]{2,1,0:T(8,128)S(1)} %broadcast_in_dim.14, s32[32]{0:T(128)} %param.21, f32[32,16,256]{2,1,0:T(8,128)} %bitcast.60), kind=kCustom, calls=%fused_computation.3 | custom fusion | flops 131072 | bytes 1572992 | tf_op jit(solution)/shard_map/scatter-add | solution.py:62
  118.8 10.8 %all_to_all.135 = f32[8,16,256]{2,1,0:T(8,128)S(1)} all-to-all(f32[8,16,256]{2,1,0:T(8,128)S(1)} %scatter_fusion.1), channel_id=1, replica_groups=mesh['leaf'=8,'batch'=4] {'leaf'}, dimensions={0} | all-to-all | bytes 262144 | tf_op jit(solution)/shard_map/all_to_all | solution.py:63
  129.6 0.2 fusion.9
  129.8 0.8 copy.39
  130.6 3.4 %all-to-all-start.4 = ((f32[1,128,256]{2,0,1:T(1,128)}), f32[1,128,256]{2,0,1:T(1,128)S(1)}, u32[]{:S(2)}, u32[]{:S(2)}) async-start(f32[1,128,256]{2,0,1:T(1,128)} %copy.39), calls=%async_computation.4 | async-start | bytes 262144 | tf_op jit(solution)/shard_map/all_to_all | solution.py:65
  134.0 0.7 compare_select_fusion.1
  134.6 6.6 %all-to-all-done.4 = f32[1,128,256]{2,0,1:T(1,128)S(1)} async-done(((f32[1,128,256]{2,0,1:T(1,128)}), f32[1,128,256]{2,0,1:T(1,128)S(1)}, u32[]{:S(2)}, u32[]{:S(2)}) %all-to-all-start.4) | async-done | bytes 131104 | tf_op jit(solution)/shard_map/all_to_all | solution.py:65
  141.3 1.4 gather_fusion
  142.6 15.1 %all_to_all.136 = f32[32,16,256]{2,1,0:T(8,128)S(1)} all-to-all(f32[32,16,256]{2,1,0:T(8,128)} %gather_fusion), channel_id=1, replica_groups=mesh['leaf'=8,'batch'=4] {'leaf'}, dimensions={0} | all-to-all | bytes 1048576 | tf_op jit(solution)/shard_map/all_to_all | solution.py:66
  157.8 0.1 fusion.17
  157.9 0.2 exponential_convert_fusion.2
  158.1 0.7 copy-done.3
  158.8 0.2 copy-done.6
  159.0 0.4 multiply_reduce_fusion
  159.4 1.1 copy.41
  160.5 3.7 %all-to-all-start.6 = ((f32[4,128,256]{2,0,1:T(4,128)}), f32[4,128,256]{2,0,1:T(4,128)S(1)}, u32[]{:S(2)}, u32[]{:S(2)}) async-start(f32[4,128,256]{2,0,1:T(4,128)} %copy.41), calls=%async_computation.6 | async-start | bytes 1048576 | tf_op jit(solution)/shard_map/all_to_all | solution.py:70
  164.2 13.3 %all-to-all-done.6 = f32[4,128,256]{2,0,1:T(4,128)S(1)} async-done(((f32[4,128,256]{2,0,1:T(4,128)}), f32[4,128,256]{2,0,1:T(4,128)S(1)}, u32[]{:S(2)}, u32[]{:S(2)}) %all-to-all-start.6) | async-done | bytes 524320 | tf_op jit(solution)/shard_map/all_to_all | solution.py:70
  177.5 0.1 copy.42
  177.6 1.8 gather_fusion.1
  179.4 4.4 %all-to-all-start.7 = ((f32[80,16,256]{2,1,0:T(8,128)}), f32[80,16,256]{2,1,0:T(8,128)}, u32[]{:S(2)}, u32[]{:S(2)}) async-start(f32[80,16,256]{2,1,0:T(8,128)} %gather_fusion.1), calls=%async_computation.7 | async-start | bytes 2621440 | tf_op jit(solution)/shard_map/all_to_all | solution.py:71
  183.8 0.0 reduce-scatter.5.cloned.1.call-start
  183.8 2.5 convolution_multiply_fusion.1
  186.4 0.0 reduce-scatter.3.cloned.1.call-start
  186.4 27.7 %all-to-all-done.7 = f32[80,16,256]{2,1,0:T(8,128)} async-done(((f32[80,16,256]{2,1,0:T(8,128)}), f32[80,16,256]{2,1,0:T(8,128)}, u32[]{:S(2)}, u32[]{:S(2)}) %all-to-all-start.7) | async-done | bytes 1310752 | tf_op jit(solution)/shard_map/all_to_all | solution.py:71
  214.2 1.4 copy.44
  215.6 0.3 fusion.12
  215.9 0.4 exponential_convert_fusion
  216.3 5.5 %convert_multiply_fusion = f32[10,256,256]{2,1,0:T(8,128)} fusion(bf16[10,256,256]{2,1,0:T(8,128)(2,1)} %param.17, bf16[10,128,256]{2,1,0:T(8,128)(2,1)S(1)} %exponential_convert_fusion, f32[10,128,256]{2,1,0:T(8,128)} %copy-done.1, f32[10,128]{1,0:T(8,128)S(1)} %get-tuple-element.4), kind=kOutput, calls=%fused_computation.6 | convolution fusion | flops 339805696 | bytes 5903360 | tf_op jit(solution)/shard_map/nbi,nbj->nij/dot_general | solution.py:28
  221.8 0.0 reduce-scatter.5.cloned.1.call-done
  221.9 1.8 fusion.7
  223.7 31.8 %reduce-scatter.3.cloned.1.call-done = f32[10,64,256]{2,1,0:T(8,128)} async-done(((f32[10,256,256]{2,1,0:T(8,128)}), f32[10,64,256]{2,1,0:T(8,128)}) %reduce-scatter.3.cloned.1.call-update) | async-done | bytes 655376 | tf_op jit(solution)/shard_map/reduce_scatter | solution.py:75
  255.5 2.3 fusion.5
  (36 shorter events, 0.3 us)
Async XLA Ops:
  7.2 1.3 copy-start
  7.2 3.9 %copy-start.7 = (bf16[10,256,256]{2,1,0:T(8,128)(2,1)S(1)}, bf16[10,256,256]{2,1,0:T(8,128)(2,1)}, u32[]{:S(2)}) copy-start(bf16[10,256,256]{2,1,0:T(8,128)(2,1)} %param.17) | copy-start | bytes 3932164
  10.0 1.1 copy-start.1
  68.0 1.9 copy-start.13
  77.5 17.7 %copy-start.8 = (bf16[4,256,256]{2,1,0:T(8,128)(2,1)S(1)}, bf16[4,256,256]{2,1,0:T(8,128)(2,1)}, u32[]{:S(2)}) copy-start(bf16[4,256,256]{2,1,0:T(8,128)(2,1)} %param.15) | copy-start | bytes 1572868
  77.5 17.7 %copy-start.11 = (s32[4,128]{1,0:T(4,128)S(1)}, s32[4,128]{1,0:T(4,128)}, u32[]{:S(2)}) copy-start(s32[4,128]{1,0:T(4,128)} %param.12) | copy-start | bytes 6148
  95.2 1.0 copy-start.5
  95.6 1.3 copy-start.2
  114.4 15.1 %copy-start.9 = (f32[1,128,256]{2,1,0:T(8,128)S(1)}, f32[1,128,256]{2,1,0:T(8,128)}, u32[]{:S(2)}) copy-start(f32[1,128,256]{2,1,0:T(8,128)} %param.19) | copy-start | bytes 393220
  114.4 15.1 %copy-start.10 = (bf16[1,256,256]{2,1,0:T(8,128)(2,1)S(1)}, bf16[1,256,256]{2,1,0:T(8,128)(2,1)}, u32[]{:S(2)}) copy-start(bf16[1,256,256]{2,1,0:T(8,128)(2,1)} %param.16) | copy-start | bytes 393220
  114.5 15.1 %copy-start.12 = (s32[1,128]{1,0:T(1,128)S(1)}, s32[1,128]{1,0:T(1,128)}, u32[]{:S(2)}) copy-start(s32[1,128]{1,0:T(1,128)} %param.13) | copy-start | bytes 1540
  130.6 10.7 %all-to-all-start.4 = ((f32[1,128,256]{2,0,1:T(1,128)}), f32[1,128,256]{2,0,1:T(1,128)S(1)}, u32[]{:S(2)}, u32[]{:S(2)}) async-start(f32[1,128,256]{2,0,1:T(1,128)} %copy.39), calls=%async_computation.4 | async-start | bytes 262144 | tf_op jit(solution)/shard_map/all_to_all | solution.py:65
  157.8 1.0 copy-start.3
  157.8 1.2 copy-start.6
  159.4 4.8 %copy-start.14 = (s32[80]{0:T(128)S(1)}, s32[80]{0:T(128)}, u32[]{:S(2)}) copy-start(s32[80]{0:T(128)} %param.20) | copy-start | bytes 964
  160.5 17.0 %all-to-all-start.6 = ((f32[4,128,256]{2,0,1:T(4,128)}), f32[4,128,256]{2,0,1:T(4,128)S(1)}, u32[]{:S(2)}, u32[]{:S(2)}) async-start(f32[4,128,256]{2,0,1:T(4,128)} %copy.41), calls=%async_computation.6 | async-start | bytes 1048576 | tf_op jit(solution)/shard_map/all_to_all | solution.py:70
  179.4 4.4 %copy-start.4 = (f32[4,128,256]{2,1,0:T(8,128)S(1)}, f32[4,128,256]{2,1,0:T(8,128)}, u32[]{:S(2)}) copy-start(f32[4,128,256]{2,1,0:T(8,128)} %copy-done.2) | copy-start | bytes 1572868
  179.4 34.8 %all-to-all-start.7 = ((f32[80,16,256]{2,1,0:T(8,128)}), f32[80,16,256]{2,1,0:T(8,128)}, u32[]{:S(2)}, u32[]{:S(2)}) async-start(f32[80,16,256]{2,1,0:T(8,128)} %gather_fusion.1), calls=%async_computation.7 | async-start | bytes 2621440 | tf_op jit(solution)/shard_map/all_to_all | solution.py:71
  183.8 38.1 %reduce-scatter.5.cloned.1.call-start = ((), (), s32[]{:S(2)}) async-start(), calls=%async_computation.11 | async-start | bytes 1310720 | tf_op jit(solution)/shard_map/reduce_scatter | solution.py:68
  186.4 69.1 %reduce-scatter.3.cloned.1.call-start = ((), (), s32[]{:S(2)}) async-start(), calls=%async_computation.10 | async-start | bytes 3276800 | tf_op jit(solution)/shard_map/reduce_scatter | solution.py:75
Sparse Core Ops, SparseCore 0:
  187.1 26.2 reduce-scatter.4
  221.9 33.4 reduce-scatter.2
where the time goes:
time: 266 us; the launch traced here: 265 us
  blocking collectives  116 us (44%)
  waiting for transfers between devices  79.4 us (30%)
  other arithmetic  16.9 us (6%)
  local copies, waits for them, and re-layouts  14.5 us (5%)
  between operations  14.3 us (5%)
  matrix products  11.7 us (4%)
  starting transfers between devices  11.5 us (4%)
    all_to_all x1, blocking collectives, body(): lax.all_to_all(up_low, 'leaf', split_axis=1, concat_axis=0, tiled=True)  55.3 us
    reduce_scatter x1, waiting for transfers between devices, body(): lax.psum_scatter(counts_low, 'batch', scatter_dimension=1, tiled=True)  31.8 us
    all_to_all x1, waiting for transfers between devices, body(): lax.all_to_all(spread_mid[parent_low], 'leaf', split_axis=0, concat_axis=...  27.7 us
    all_to_all x1, blocking collectives, body(): lax.all_to_all(gathered_mid, 'leaf', split_axis=0, concat_axis=1, tiled=T...  17.7 us
    all_to_all x1, blocking collectives, body(): lax.all_to_all(up_mid, 'leaf', split_axis=1, concat_axis=0, tiled=True)  17.4 us
    all_to_all x1, blocking collectives, body(): lax.all_to_all(spread_top[parent_mid], 'leaf', split_axis=0, concat_axis=...  15.1 us
    all_to_all x1, waiting for transfers between devices, body(): lax.all_to_all(total_mid, 'leaf', split_axis=1, concat_axis=0, tiled=True)  13.3 us
    all_to_all x1, blocking collectives, body(): lax.all_to_all(gathered_top, 'leaf', split_axis=0, concat_axis=1, tiled=T...  10.8 us
  transfers between devices with their start and end apart: 5, of which 4 were waited for; matrix products, arithmetic and copies ran while one was open for 5% of the time, Pallas kernels for 0%

commit v1 on v0

--- a/solution.py
+++ b/solution.py
@@ -1,9 +1,15 @@
+import functools
+
 import jax
 import jax.numpy as jnp
 from jax import lax
+from jax.experimental import pallas as pl
+from jax.experimental.pallas import tpu as pltpu
 from jax.sharding import PartitionSpec as P
 
 PSEUDO = 0.001
+REMOTE = 3
+MESH = pl.DeviceIdType.MESH
 
 
 def lookup_all(table, pixels):
@@ -76,9 +82,381 @@
     return (update_low, update_mid)
 
 
+def dot(a, b, left, right):
+    return lax.dot_general(
+        a, b, (((left,), (right,)), ((), ())), preferred_element_type=jnp.float32
+    )
+
+
+def kernel(
+    leaves,
+    parts,
+    offsets,
+    meta,
+    pixels_low,
+    pixels_mid,
+    pixels_top,
+    emit_low,
+    emit_mid,
+    emit_top,
+    trans_low,
+    trans_mid,
+    outside_top,
+    update_low,
+    update_mid,
+    pix,
+    edge_top,
+    own_top,
+    far_up,
+    far_slices,
+    mid_send,
+    mid_sums,
+    scaled_low,
+    linear_low,
+    up_mid,
+    up_slices,
+    totals,
+    total_send,
+    total_mine,
+    scaled_mid,
+    linear_mid,
+    post_mid,
+    post_slices,
+    post_send,
+    post,
+    counts_mid,
+    counts_own,
+    send_sem,
+    recv_sem,
+):
+    at_parent_low, at_parent_mid, at_index, at_parent, at_place = offsets
+    leaf = lax.axis_index("leaf")
+    part = lax.axis_index("batch")
+    devices = leaves * parts
+    me = leaf * parts + part
+    low_count = pixels_low.shape[0]
+    mid_count = pixels_mid.shape[0]
+    images = pixels_low.shape[1]
+    states = trans_low.shape[2]
+    share_rows = states // parts
+    rows = states // devices
+
+    def slice_of(l, q):
+        return pl.ds(pl.multiple_of(q * share_rows + l * rows, rows), rows)
+
+    def quarter_of(q):
+        return pl.ds(pl.multiple_of(q * share_rows, share_rows), share_rows)
+
+    def send(src, dst, phase, l, q):
+        pltpu.make_async_remote_copy(
+            src_ref=src,
+            dst_ref=dst,
+            send_sem=send_sem.at[phase],
+            recv_sem=recv_sem.at[phase],
+            device_id=(l, q),
+            device_id_type=MESH,
+        ).start()
+
+    def wait_recv(ref, phase):
+        pltpu.make_async_copy(ref, ref, recv_sem.at[phase]).wait()
+
+    def wait_send(ref, phase):
+        pltpu.make_async_copy(ref, ref, send_sem.at[phase]).wait()
+
+    def each_other(step):
+        def one(k, carry):
+            t = lax.rem(me + k, devices)
+            step(t, lax.div(t, parts), lax.rem(t, parts))
+            return carry
+
+        lax.fori_loop(1, devices, one, 0)
+
+    def each_leaf(step):
+        def one(k, carry):
+            step(lax.rem(leaf + k, leaves))
+            return carry
+
+        lax.fori_loop(1, leaves, one, 0)
+
+    def each_part(step):
+        def one(k, carry):
+            step(lax.rem(part + k, parts))
+            return carry
+
+        lax.fori_loop(1, parts, one, 0)
+
+    barrier = pltpu.get_barrier_semaphore()
+
+    def greet(t, l, q):
+        pl.semaphore_signal(barrier, inc=1, device_id=(l, q), device_id_type=MESH)
+
+    each_other(greet)
+
+    levels = lax.broadcasted_iota(jnp.int32, (emit_low.shape[1], images), 0)
+
+    def picks(row):
+        return jnp.where(levels == row, 1.0, 0.0).astype(jnp.bfloat16)
+
+    pix[part, 0:low_count, :] = pixels_low[...]
+    pix[part, low_count : low_count + mid_count, :] = pixels_mid[...]
+    own_top[...] = dot(emit_top[0], picks(pixels_top[...]), 0, 0) + outside_top[0].T
+    pl.semaphore_wait(barrier, devices - 1)
+
+    each_part(lambda q: send(pix.at[part], pix.at[part], 0, leaf, q))
+    mine = pl.ds(pl.multiple_of(part * images, images), images)
+    each_other(
+        lambda t, l, q: send(
+            own_top.at[slice_of(l, q)], edge_top.at[leaf, :, mine], 1, l, q
+        )
+    )
+    edge_top[leaf, :, mine] = own_top[slice_of(leaf, part), :]
+    wait_recv(pix.at[pl.ds(0, parts - 1)], 0)
+
+    def lookup(table, node):
+        chosen = jnp.concatenate(
+            [picks(pix[q, pl.ds(node, 1), :]) for q in range(parts)], axis=1
+        )
+        return dot(table, chosen, 0, 0)
+
+    def scale(inside):
+        return jnp.exp(inside - jnp.max(inside, axis=0, keepdims=True))
+
+    def far(s, carry):
+        node = meta[at_index + leaf * REMOTE + s]
+        scaled = scale(lookup(emit_low[node], node)).astype(jnp.bfloat16)
+        far_up[s] = jnp.log(dot(trans_low[node], scaled, 1, 0))
+        return carry
+
+    lax.fori_loop(0, REMOTE, far, 0)
+    each_leaf(
+        lambda l: send(
+            far_up.at[:, slice_of(l, part), :], far_slices.at[leaf], 2, l, part
+        )
+    )
+    far_slices[leaf] = far_up[:, slice_of(leaf, part), :]
+
+    total_mine[...] = lookup(emit_mid[part], low_count + part)
+
+    def near(c, carry):
+        scaled = scale(lookup(emit_low[c], c)).astype(jnp.bfloat16)
+        scaled_low[c] = scaled
+        linear = dot(trans_low[c], scaled, 1, 0)
+        linear_mid[...] = linear
+        linear_low[c] = linear_mid[quarter_of(part), :]
+        weight = jnp.where(meta[at_parent_low + leaf * low_count + c] == me, 1.0, 0.0)
+        total_mine[...] += weight * jnp.log(linear)
+        return carry
+
+    lax.fori_loop(0, low_count, near, 0)
+    wait_recv(far_slices.at[pl.ds(0, leaves - 1)], 2)
+
+    def sum_far(t):
+        total = jnp.zeros(mid_send.shape[1:], jnp.float32)
+        for l in range(leaves):
+            for s in range(REMOTE):
+                weight = jnp.where(meta[at_parent + l * REMOTE + s] == t, 1.0, 0.0)
+                total += weight * far_slices[l, s]
+        return total
+
+    def send_sum(t, l, q):
+        mid_send[t] = sum_far(t)
+        send(mid_send.at[t], mid_sums.at[slice_of(leaf, part)], 3, l, q)
+
+    each_other(send_sum)
+    mid_sums[slice_of(leaf, part), :] = sum_far(me)
+    wait_recv(mid_sums.at[pl.ds(0, states - rows)], 3)
+
+    exact = scale(total_mine[...] + mid_sums[...])
+    post_mid[...] = exact
+    scaled_mid[...] = exact.astype(jnp.bfloat16)
+    linear = dot(trans_mid[part], scaled_mid[...], 1, 0)
+    linear_mid[...] = linear
+    up_mid[...] = jnp.log(linear)
+    each_other(lambda t, l, q: send(up_mid.at[slice_of(l, q)], up_slices.at[me], 4, l, q))
+    up_slices[me] = up_mid[slice_of(leaf, part), :]
+    wait_recv(own_top.at[pl.ds(0, states - rows)], 1)
+    wait_recv(up_slices.at[pl.ds(0, devices - 1)], 4)
+
+    def top(r, carry):
+        total = edge_top[r]
+        for p in range(devices):
+            weight = jnp.where(meta[at_parent_mid + p] == r, 1.0, 0.0)
+            total += weight * up_slices[p]
+        totals[r] = total
+        return carry
+
+    lax.fori_loop(0, leaves, top, 0)
+
+    def send_total(t, l, q):
+        total_send[t] = totals[meta[at_parent_mid + t]]
+        send(total_send.at[t], total_mine.at[slice_of(leaf, part)], 5, l, q)
+
+    each_other(send_total)
+    total_mine[slice_of(leaf, part), :] = totals[meta[at_parent_mid + me]]
+    wait_recv(total_mine.at[pl.ds(0, states - rows)], 5)
+
+    reached = scale(total_mine[...])
+    share = (
+        reached / (linear_mid[...] * jnp.sum(reached, axis=0, keepdims=True))
+    ).astype(jnp.bfloat16)
+    posterior = post_mid[...] * dot(trans_mid[part], share, 0, 0)
+    post_mid[...] = posterior / jnp.sum(posterior, axis=0, keepdims=True)
+    each_other(
+        lambda t, l, q: send(post_mid.at[slice_of(l, q)], post_slices.at[me], 6, l, q)
+    )
+    each_part(lambda q: send(post_mid.at[quarter_of(q)], post.at[part], 7, leaf, q))
+    post_slices[me] = post_mid[slice_of(leaf, part), :]
+    post[part] = post_mid[quarter_of(part), :]
+
+    def finished(share, scaled, weight):
+        counts = dot(share, scaled, 1, 1) * weight.astype(jnp.float32) + PSEUDO
+        return states * counts / jnp.sum(counts, axis=-1, keepdims=True)
+
+    counts_own[...] = finished(share, scaled_mid[...], trans_mid[part])
+    each_part(lambda q: send(counts_own.at[quarter_of(q)], counts_mid.at[part], 8, leaf, q))
+    counts_mid[part] = counts_own[quarter_of(part), :]
+    wait_recv(post_slices.at[pl.ds(0, devices - 1)], 6)
+
+    def pick(l):
+        for s in range(REMOTE):
+            post_send[l, s] = post_slices[jnp.maximum(meta[at_parent + l * REMOTE + s], 0)]
+
+    landing = pl.ds(pl.multiple_of(leaf * rows, rows), rows)
+
+    def send_pick(l):
+        pick(l)
+        send(post_send.at[l], post.at[pl.ds(mid_count, REMOTE), landing], 9, l, part)
+
+    each_leaf(send_pick)
+    pick(leaf)
+    post[mid_count : mid_count + REMOTE, landing, :] = post_send[leaf]
+    wait_recv(post.at[pl.ds(0, parts - 1)], 7)
+    wait_recv(post_send.at[pl.ds(0, leaves - 1)], 9)
+
+    def low_update(c, carry):
+        share = (post[meta[at_place + leaf * low_count + c]] / linear_low[c]).astype(
+            jnp.bfloat16
+        )
+        update_low[c] = finished(share, scaled_low[c], trans_low[c, quarter_of(part), :])
+        return carry
+
+    lax.fori_loop(0, low_count, low_update, 0)
+    wait_recv(counts_mid.at[pl.ds(0, parts - 1)], 8)
+    update_mid[...] = counts_mid[...]
+
+    wait_send(pix.at[pl.ds(0, parts - 1)], 0)
+    wait_send(own_top.at[pl.ds(0, states - rows)], 1)
+    wait_send(far_slices.at[pl.ds(0, leaves - 1)], 2)
+    wait_send(mid_send.at[pl.ds(0, devices - 1)], 3)
+    wait_send(up_slices.at[pl.ds(0, devices - 1)], 4)
+    wait_send(total_send.at[pl.ds(0, devices - 1)], 5)
+    wait_send(post_slices.at[pl.ds(0, devices - 1)], 6)
+    wait_send(post.at[pl.ds(0, parts - 1)], 7)
+    wait_send(counts_mid.at[pl.ds(0, parts - 1)], 8)
+    wait_send(post_send.at[pl.ds(0, leaves - 1)], 9)
+
+
+def plan(parent_low, parent_mid, leaves, low_count, mid_count):
+    parents = parent_low.reshape(leaves, low_count)
+    nodes = jnp.arange(low_count, dtype=jnp.int32)
+    far = parents // mid_count != jnp.arange(leaves, dtype=jnp.int32)[:, None]
+    before = far[:, None, :] & (nodes[None, :] < nodes[:, None])[None]
+    rank = jnp.sum(before.astype(jnp.int32), axis=-1)
+    slots = jnp.arange(REMOTE, dtype=jnp.int32)[None, :, None]
+    chosen = far[:, None, :] & (rank[:, None, :] == slots)
+    index = jnp.sum(jnp.where(chosen, nodes, 0), axis=-1)
+    parent = jnp.sum(jnp.where(chosen, parents[:, None, :] + 1, 0), axis=-1) - 1
+    place = jnp.where(far, mid_count + rank, parents % mid_count)
+    pieces = [parent_low, parent_mid, index.reshape(-1), parent.reshape(-1), place.reshape(-1)]
+    offsets = [0]
+    for piece in pieces[:-1]:
+        offsets.append(offsets[-1] + piece.shape[0])
+    return jnp.concatenate(pieces), tuple(offsets)
+
+
+def fused(
+    leaves,
+    parts,
+    pixels_low,
+    pixels_mid,
+    pixels_top,
+    emit_low,
+    emit_mid,
+    emit_top,
+    trans_low,
+    trans_mid,
+    outside_top,
+    parent_low,
+    parent_mid,
+):
+    low_count, images = pixels_low.shape
+    mid_count = pixels_mid.shape[0]
+    states = trans_low.shape[2]
+    devices = leaves * parts
+    share_rows = states // parts
+    rows = states // devices
+    whole = images * parts
+    meta, offsets = plan(parent_low, parent_mid, leaves, low_count, mid_count)
+    held = -(-(low_count + mid_count) // 8) * 8
+    real = jnp.float32
+    return pl.pallas_call(
+        functools.partial(kernel, leaves, parts, offsets),
+        out_shape=(
+            jax.ShapeDtypeStruct((low_count, share_rows, states), real),
+            jax.ShapeDtypeStruct((mid_count, share_rows, states), real),
+        ),
+        in_specs=[pl.BlockSpec(memory_space=pltpu.SMEM)]
+        + [pl.BlockSpec(memory_space=pltpu.VMEM)] * 9,
+        out_specs=(pl.BlockSpec(memory_space=pltpu.VMEM),) * 2,
+        scratch_shapes=[
+            pltpu.VMEM((parts, held, images), jnp.int32),
+            pltpu.VMEM((leaves, rows, whole), real),
+            pltpu.VMEM((states, images), real),
+            pltpu.VMEM((REMOTE, states, whole), real),
+            pltpu.VMEM((leaves, REMOTE, rows, whole), real),
+            pltpu.VMEM((devices, rows, whole), real),
+            pltpu.VMEM((states, whole), real),
+            pltpu.VMEM((low_count, states, whole), jnp.bfloat16),
+            pltpu.VMEM((low_count, share_rows, whole), real),
+            pltpu.VMEM((states, whole), real),
+            pltpu.VMEM((devices, rows, whole), real),
+            pltpu.VMEM((leaves, rows, whole), real),
+            pltpu.VMEM((devices, rows, whole), real),
+            pltpu.VMEM((states, whole), real),
+            pltpu.VMEM((states, whole), jnp.bfloat16),
+            pltpu.VMEM((states, whole), real),
+            pltpu.VMEM((states, whole), real),
+            pltpu.VMEM((devices, rows, whole), real),
+            pltpu.VMEM((leaves, REMOTE, rows, whole), real),
+            pltpu.VMEM((mid_count + REMOTE, share_rows, whole), real),
+            pltpu.VMEM((mid_count, share_rows, states), real),
+            pltpu.VMEM((states, states), real),
+            pltpu.SemaphoreType.DMA((10,)),
+            pltpu.SemaphoreType.DMA((10,)),
+        ],
+        compiler_params=pltpu.CompilerParams(
+            collective_id=0, has_side_effects=True, vmem_limit_bytes=48 * 2**20
+        ),
+    )(
+        meta,
+        pixels_low,
+        pixels_mid,
+        pixels_top,
+        emit_low,
+        emit_mid,
+        emit_top,
+        trans_low,
+        trans_mid,
+        outside_top,
+    )
+
+
 def solution(mesh):
+    leaves, parts = mesh.shape["leaf"], mesh.shape["batch"]
+    fits = 256 % (8 * leaves * parts) == 0
+    chosen = functools.partial(fused, leaves, parts) if fits else body
     return jax.shard_map(
-        body,
+        chosen,
         mesh=mesh,
         in_specs=(
             P("leaf", "batch"),

time: 266 us -> 98.8 us (0.37)
  blocking collectives: 116 us -> 0 us
  Pallas kernels: 0 us -> 84.2 us
  waiting for transfers between devices: 79.4 us -> 0 us
  other arithmetic: 16.9 us -> 1.14 us
  between operations: 14.3 us -> 0.69 us
  matrix products: 11.7 us -> 0 us
  starting transfers between devices: 11.5 us -> 0 us
    all_to_all x5 -> x0, blocking collectives: 116 us -> none  [the longest x1 55.3 us: body(): lax.all_to_all(up_low, 'leaf', split_axis=1, concat_axis=0, tiled=True)]
    pallas_call x0 -> x1, Pallas kernels: none -> 84.2 us  [fused(): pl.pallas_call(functools.partial(kernel, leaves, parts, offsets), out_sha...]
    all_to_all x3 -> x0, waiting for transfers between devices: 47.6 us -> none  [the longest x1 27.7 us: body(): lax.all_to_all(spread_mid[parent_low], 'leaf', split_axis=0, concat_axis=...]
    reduce_scatter x2 -> x0, waiting for transfers between devices: 31.8 us -> none  [the longest x1 31.8 us: body(): lax.psum_scatter(counts_low, 'batch', scatter_dimension=1, tiled=True)]
    dot_general x8 -> x0, matrix products: 11.7 us -> none  [the longest x2 8.04 us: edge_all(): jnp.einsum('nbi,nbj->nij', share, scaled, preferred_element_type=jnp.floa...]
    all_to_all x3 -> x0, starting transfers between devices: 11.4 us -> none  [the longest x1 4.39 us: body(): lax.all_to_all(spread_mid[parent_low], 'leaf', split_axis=0, concat_axis=...]
    scatter-add x2 -> x0, other arithmetic: 11 us -> none  [the longest x1 7.56 us: body(): jax.ops.segment_sum(moved, parent_low, num_segments=mid_count * devices)]
    unnamed x31 -> x20, local copies, waits for them, and re-layouts: 3.9 us -> 10.1 us
  transfers between devices with their start and end apart: 5 -> 0, of which waited for: 4 -> 0; matrix products, arithmetic and copies ran while one was open for 5% -> 0% of each run, Pallas kernels for 0% -> 0%
where the time goes in v1:
time: 98.8 us; the launch traced here: 98.2 us
  Pallas kernels  84.2 us (85%)
  local copies, waits for them, and re-layouts  12.1 us (12%)
  other arithmetic  1.14 us (1%)
    pallas_call x1, Pallas kernels, fused(): pl.pallas_call(functools.partial(kernel, leaves, parts, offsets), out_sha...  84.2 us
    unnamed x20, local copies, waits for them, and re-layouts  10.1 us

profile of v1, /device:TPU:0, one launch (start us, length us, event | category | flops | bytes accessed | tf_op | source)
XLA Modules:
  0.0 98.2 jit_solution(18026531953217938831)
XLA Ops:
  0.6 0.7 reshape.73
  1.4 0.1 ne.66
  1.5 0.3 convert_reduce_fusion
  1.8 0.1 copy.17
  1.8 0.2 select_reduce_fusion
  2.0 0.1 add.35
  2.1 0.7 compare_select_fusion
  2.8 0.1 copy.19
  2.9 0.1 sub.15
  2.9 0.1 copy.18
  3.0 0.1 reshape.74
  3.1 0.8 concatenate.3.meta
  3.9 0.0 copy-start
  3.9 1.3 %copy-done = bf16[10,256,256]{2,1,0:T(8,128)(2,1)S(1)} copy-done((bf16[10,256,256]{2,1,0:T(8,128)(2,1)S(1)}, bf16[10,256,256]{2,1,0:T(8,128)(2,1)}, u32[]{:S(2)}) %copy-start) | copy-done | bytes 1310744
  5.2 0.0 copy-start.1
  5.2 1.3 %copy-done.1 = bf16[10,256,256]{2,1,0:T(8,128)(2,1)S(1)} copy-done((bf16[10,256,256]{2,1,0:T(8,128)(2,1)S(1)}, bf16[10,256,256]{2,1,0:T(8,128)(2,1)}, u32[]{:S(2)}) %copy-start.1) | copy-done | bytes 1310744
  6.5 0.0 copy-start.2
  6.5 1.0 %copy-done.2 = bf16[4,256,256]{2,1,0:T(8,128)(2,1)S(1)} copy-done((bf16[4,256,256]{2,1,0:T(8,128)(2,1)S(1)}, bf16[4,256,256]{2,1,0:T(8,128)(2,1)}, u32[]{:S(2)}) %copy-start.2) | copy-done | bytes 524312
  7.5 0.0 copy-start.3
  7.5 1.0 %copy-done.3 = bf16[4,256,256]{2,1,0:T(8,128)(2,1)S(1)} copy-done((bf16[4,256,256]{2,1,0:T(8,128)(2,1)S(1)}, bf16[4,256,256]{2,1,0:T(8,128)(2,1)}, u32[]{:S(2)}) %copy-start.3) | copy-done | bytes 524312
  8.6 0.0 copy-start.4
  8.6 0.9 copy-done.4
  9.5 0.0 copy-start.5
  9.5 0.9 copy-done.5
  10.4 0.0 copy-start.6
  10.4 0.7 copy-done.6
  11.1 0.0 copy-start.7
  11.1 0.7 copy-done.7
  11.8 0.0 copy-start.8
  11.8 0.7 copy-done.8
  12.4 84.2 %shard_map.122 = (f32[10,64,256]{2,1,0:T(8,128)S(1)}, f32[4,64,256]{2,1,0:T(8,128)S(1)}) custom-call(s32[240]{0:T(256)S(1)} %concatenate.3.meta, s32[10,128]{1,0:T(8,128)S(1)} %copy-done.6, s32[4,128]{1,0:T(4,128)S(1)} %copy-done.7, s32[1,128]{1,0:T(1,128)S(1)} %copy-done.8, bf16[10,256,256]{2,1,0:T(8,128)(2,1)S(1)} %copy-done, ...), custom_call_target="tpu_custom_call" | custom-call | tf_op jit(solution)/shard_map/pallas_call | solution.py:402
  96.7 0.8 copy.23
  97.5 0.7 copy.24
  (6 shorter events, 0.0 us)
Async XLA Ops:
  3.9 1.3 %copy-start = (bf16[10,256,256]{2,1,0:T(8,128)(2,1)S(1)}, bf16[10,256,256]{2,1,0:T(8,128)(2,1)}, u32[]{:S(2)}) copy-start(bf16[10,256,256]{2,1,0:T(8,128)(2,1)} %emit_low.1) | copy-start | bytes 3932164
  5.2 1.3 %copy-start.1 = (bf16[10,256,256]{2,1,0:T(8,128)(2,1)S(1)}, bf16[10,256,256]{2,1,0:T(8,128)(2,1)}, u32[]{:S(2)}) copy-start(bf16[10,256,256]{2,1,0:T(8,128)(2,1)} %trans_low.1) | copy-start | bytes 3932164
  6.5 1.0 %copy-start.2 = (bf16[4,256,256]{2,1,0:T(8,128)(2,1)S(1)}, bf16[4,256,256]{2,1,0:T(8,128)(2,1)}, u32[]{:S(2)}) copy-start(bf16[4,256,256]{2,1,0:T(8,128)(2,1)} %emit_mid.1) | copy-start | bytes 1572868
  7.5 1.0 %copy-start.3 = (bf16[4,256,256]{2,1,0:T(8,128)(2,1)S(1)}, bf16[4,256,256]{2,1,0:T(8,128)(2,1)}, u32[]{:S(2)}) copy-start(bf16[4,256,256]{2,1,0:T(8,128)(2,1)} %trans_mid.1) | copy-start | bytes 1572868
  8.6 0.9 copy-start.4
  9.5 0.9 copy-start.5
  10.4 0.7 copy-start.6
  11.1 0.7 copy-start.7
  11.8 0.7 copy-start.8

commit v2 on v0

--- a/solution.py
+++ b/solution.py
@@ -1,9 +1,17 @@
+import functools
+
 import jax
 import jax.numpy as jnp
 from jax import lax
+from jax.experimental import pallas as pl
+from jax.experimental.pallas import tpu as pltpu
 from jax.sharding import PartitionSpec as P
 
 PSEUDO = 0.001
+REMOTE = 3
+HALVES = 1
+STRIDE = 13
+MESH = pl.DeviceIdType.MESH
 
 
 def lookup_all(table, pixels):
@@ -76,9 +84,503 @@
     return (update_low, update_mid)
 
 
+def dot(a, b, left, right):
+    return lax.dot_general(
+        a, b, (((left,), (right,)), ((), ())), preferred_element_type=jnp.float32
+    )
+
+
+def kernel(
+    leaves,
+    parts,
+    parent_low,
+    parent_mid,
+    pixels_low_hbm,
+    pixels_mid_hbm,
+    pixels_top_hbm,
+    emit_low_hbm,
+    emit_mid_hbm,
+    emit_top_hbm,
+    trans_low_hbm,
+    trans_mid_hbm,
+    outside_top_hbm,
+    update_low,
+    update_mid,
+    far_index,
+    far_parent,
+    place,
+    pixels_low,
+    pixels_mid,
+    pixels_top,
+    emit_low,
+    emit_mid,
+    emit_top,
+    trans_low,
+    trans_mid,
+    outside_top,
+    pix,
+    edge_top,
+    own_top,
+    far_up,
+    far_slices,
+    mid_send,
+    mid_sums,
+    inside_own,
+    scaled_low,
+    linear_low,
+    linear_full,
+    up_mid,
+    up_slices,
+    totals,
+    total_send,
+    total_mine,
+    scaled_mid,
+    linear_mid,
+    share_mid,
+    post_mid,
+    post_slices,
+    post_send,
+    post_near,
+    post_far,
+    counts_mid,
+    counts_own,
+    far_counts,
+    send_sem,
+    recv_sem,
+    load_sem,
+):
+    leaf = lax.axis_index("leaf")
+    part = lax.axis_index("batch")
+    devices = leaves * parts
+    me = leaf * parts + part
+    low_count = pixels_low.shape[0]
+    mid_count = pixels_mid.shape[0]
+    images = pixels_low.shape[1]
+    states = trans_low.shape[2]
+    share_rows = states // parts
+    rows = states // devices
+    wide = images * parts // HALVES
+
+    loads = [
+        pltpu.make_async_copy(source, target, load_sem.at[i])
+        for i, (source, target) in enumerate(
+            (
+                (pixels_low_hbm, pixels_low),
+                (pixels_mid_hbm, pixels_mid),
+                (pixels_top_hbm, pixels_top),
+                (emit_top_hbm, emit_top),
+                (outside_top_hbm, outside_top),
+                (emit_low_hbm, emit_low),
+                (trans_low_hbm, trans_low),
+                (emit_mid_hbm.at[part], emit_mid),
+                (trans_mid_hbm.at[part], trans_mid),
+            )
+        )
+    ]
+    for load in loads:
+        load.start()
+
+    def slice_of(l, q):
+        return pl.ds(pl.multiple_of(q * share_rows + l * rows, rows), rows)
+
+    def quarter_of(q):
+        return pl.ds(pl.multiple_of(q * share_rows, share_rows), share_rows)
+
+    def lanes(h):
+        return pl.ds(h * wide, wide)
+
+    def send(src, dst, phase, l, q):
+        pltpu.make_async_remote_copy(
+            src_ref=src,
+            dst_ref=dst,
+            send_sem=send_sem.at[phase],
+            recv_sem=recv_sem.at[phase],
+            device_id=(l, q),
+            device_id_type=MESH,
+        ).start()
+
+    def wait_recv(ref, phase):
+        pltpu.make_async_copy(ref, ref, recv_sem.at[phase]).wait()
+
+    def wait_send(ref, phase):
+        pltpu.make_async_copy(ref, ref, send_sem.at[phase]).wait()
+
+    def each_other(step):
+        def one(k, carry):
+            t = lax.rem(me + STRIDE * k, devices)
+            step(t, lax.div(t, parts), lax.rem(t, parts))
+            return carry
+
+        lax.fori_loop(1, devices, one, 0)
+
+    def each_leaf(step):
+        def one(k, carry):
+            step(lax.rem(leaf + 3 * k, leaves))
+            return carry
+
+        lax.fori_loop(1, leaves, one, 0)
+
+    def each_part(step):
+        def one(k, carry):
+            step(lax.rem(part + k, parts))
+            return carry
+
+        lax.fori_loop(1, parts, one, 0)
+
+    barrier = pltpu.get_barrier_semaphore()
+
+    def greet(t, l, q):
+        pl.semaphore_signal(barrier, inc=1, device_id=(l, q), device_id_type=MESH)
+
+    each_other(greet)
+
+    def far_row(l, carry):
+        found = jnp.int32(0)
+        parents = [jnp.int32(-1)] * REMOTE
+        for c in range(low_count):
+            parent = parent_low[l * low_count + c]
+            away = lax.div(parent, mid_count) != l
+            for s in range(REMOTE):
+                parents[s] = jnp.where(away & (found == s), parent, parents[s])
+            found = found + jnp.where(away, 1, 0)
+        for s in range(REMOTE):
+            far_parent[l * REMOTE + s] = parents[s]
+        return carry
+
+    lax.fori_loop(0, leaves, far_row, 0)
+    found = jnp.int32(0)
+    nodes = [jnp.int32(0)] * REMOTE
+    for c in range(low_count):
+        parent = parent_low[leaf * low_count + c]
+        away = lax.div(parent, mid_count) != leaf
+        for s in range(REMOTE):
+            nodes[s] = jnp.where(away & (found == s), c, nodes[s])
+        place[c] = jnp.where(
+            away, mid_count + jnp.minimum(found, REMOTE - 1), lax.rem(parent, mid_count)
+        )
+        found = found + jnp.where(away, 1, 0)
+    for s in range(REMOTE):
+        far_index[s] = nodes[s]
+
+    levels = lax.broadcasted_iota(jnp.int32, (emit_low.shape[1], images), 0)
+
+    def picks(row):
+        return jnp.where(levels == row, 1.0, 0.0).astype(jnp.bfloat16)
+
+    loads[0].wait()
+    loads[1].wait()
+    pix[part, 0:low_count, :] = pixels_low[...]
+    pix[part, low_count : low_count + mid_count, :] = pixels_mid[...]
+    pl.semaphore_wait(barrier, devices - 1)
+    each_part(lambda q: send(pix.at[part], pix.at[part], 0, leaf, q))
+    for load in loads[2:5]:
+        load.wait()
+    own_top[...] = dot(emit_top[0], picks(pixels_top[...]), 0, 0) + outside_top[0].T
+    mine = pl.ds(pl.multiple_of(part * images, images), images)
+    each_other(
+        lambda t, l, q: send(
+            own_top.at[slice_of(l, q)], edge_top.at[leaf, :, mine], 1, l, q
+        )
+    )
+    edge_top[leaf, :, mine] = own_top[slice_of(leaf, part), :]
+    loads[5].wait()
+    loads[6].wait()
+    wait_recv(pix.at[pl.ds(0, parts - 1)], 0)
+
+    def lookup(table, node, first, last):
+        chosen = jnp.concatenate(
+            [picks(pix[q, pl.ds(node, 1), :]) for q in range(first, last)], axis=1
+        )
+        return dot(table, chosen, 0, 0)
+
+    def scale(inside):
+        return jnp.exp(inside - jnp.max(inside, axis=0, keepdims=True))
+
+    per = parts // HALVES
+    for h in range(HALVES):
+
+        def far(s, carry):
+            node = far_index[s]
+            scaled = scale(lookup(emit_low[node], node, h * per, h * per + per))
+            far_up[h, s] = jnp.log(dot(trans_low[node], scaled.astype(jnp.bfloat16), 1, 0))
+            return carry
+
+        lax.fori_loop(0, REMOTE, far, 0)
+        each_leaf(
+            lambda l: send(
+                far_up.at[h, :, slice_of(l, part), :],
+                far_slices.at[h, leaf],
+                10 + h,
+                l,
+                part,
+            )
+        )
+        far_slices[h, leaf] = far_up[h, :, slice_of(leaf, part), :]
+
+    loads[7].wait()
+    loads[8].wait()
+    inside_own[...] = lookup(emit_mid[...], low_count + part, 0, parts)
+
+    def near(c, carry):
+        scaled = scale(lookup(emit_low[c], c, 0, parts)).astype(jnp.bfloat16)
+        scaled_low[c] = scaled
+        linear = dot(trans_low[c], scaled, 1, 0)
+        linear_full[...] = linear
+        linear_low[c] = linear_full[quarter_of(part), :]
+        weight = jnp.where(parent_low[leaf * low_count + c] == me, 1.0, 0.0)
+        inside_own[...] += weight * jnp.log(linear)
+        return carry
+
+    lax.fori_loop(0, low_count // 2, near, 0)
+
+    for h in range(HALVES):
+        wait_recv(far_slices.at[h, pl.ds(0, leaves - 1)], 10 + h)
+
+        def sum_far(t):
+            total = jnp.zeros((rows, wide), jnp.float32)
+            for l in range(leaves):
+                for s in range(REMOTE):
+                    weight = jnp.where(far_parent[l * REMOTE + s] == t, 1.0, 0.0)
+                    total += weight * far_slices[h, l, s]
+            return total
+
+        def send_sum(t, l, q):
+            mid_send[h, t] = sum_far(t)
+            send(mid_send.at[h, t], mid_sums.at[h, slice_of(leaf, part)], 12 + h, l, q)
+
+        each_other(send_sum)
+        mid_sums[h, slice_of(leaf, part), :] = sum_far(me)
+
+    lax.fori_loop(low_count // 2, low_count, near, 0)
+
+    for h in range(HALVES):
+        wait_recv(mid_sums.at[h, pl.ds(0, states - rows)], 12 + h)
+        exact = scale(inside_own[:, lanes(h)] + mid_sums[h])
+        post_mid[h] = exact
+        scaled = exact.astype(jnp.bfloat16)
+        scaled_mid[:, lanes(h)] = scaled
+        linear = dot(trans_mid[...], scaled, 1, 0)
+        linear_mid[h] = linear
+        up_mid[h] = jnp.log(linear)
+        each_other(
+            lambda t, l, q: send(
+                up_mid.at[h, slice_of(l, q)], up_slices.at[h, me], 14 + h, l, q
+            )
+        )
+        up_slices[h, me] = up_mid[h, slice_of(leaf, part), :]
+
+    wait_recv(own_top.at[pl.ds(0, states - rows)], 1)
+    for h in range(HALVES):
+        wait_recv(up_slices.at[h, pl.ds(0, devices - 1)], 14 + h)
+
+        def top(r, carry):
+            total = edge_top[r, :, lanes(h)]
+            for p in range(devices):
+                weight = jnp.where(parent_mid[p] == r, 1.0, 0.0)
+                total += weight * up_slices[h, p]
+            totals[h, r] = total
+            return carry
+
+        lax.fori_loop(0, leaves, top, 0)
+
+        def send_total(t, l, q):
+            total_send[h, t] = totals[h, parent_mid[t]]
+            send(total_send.at[h, t], total_mine.at[h, slice_of(leaf, part)], 16 + h, l, q)
+
+        each_other(send_total)
+        total_mine[h, slice_of(leaf, part), :] = totals[h, parent_mid[me]]
+
+    for h in range(HALVES):
+        wait_recv(total_mine.at[h, pl.ds(0, states - rows)], 16 + h)
+        reached = scale(total_mine[h])
+        share = (
+            reached / (linear_mid[h] * jnp.sum(reached, axis=0, keepdims=True))
+        ).astype(jnp.bfloat16)
+        share_mid[:, lanes(h)] = share
+        posterior = post_mid[h] * dot(trans_mid[...], share, 0, 0)
+        post_mid[h] = posterior / jnp.sum(posterior, axis=0, keepdims=True)
+        each_other(
+            lambda t, l, q: send(
+                post_mid.at[h, slice_of(l, q)], post_slices[h].at[me], 18 + h, l, q
+            )
+        )
+        post_slices[h][me] = post_mid[h, slice_of(leaf, part), :]
+        each_part(
+            lambda q: send(
+                post_mid.at[h, quarter_of(q)], post_near.at[part, :, lanes(h)], 20 + h, leaf, q
+            )
+        )
+        post_near[part, :, lanes(h)] = post_mid[h, quarter_of(part), :]
+
+    def finished(share, scaled, weight):
+        counts = dot(share, scaled, 1, 1) * weight.astype(jnp.float32) + PSEUDO
+        return states * counts / jnp.sum(counts, axis=-1, keepdims=True)
+
+    counts_own[...] = finished(share_mid[...], scaled_mid[...], trans_mid[...])
+    each_part(lambda q: send(counts_own.at[quarter_of(q)], counts_mid.at[part], 2, leaf, q))
+    counts_mid[part] = counts_own[quarter_of(part), :]
+
+    landing = pl.ds(pl.multiple_of(leaf * rows, rows), rows)
+    for h in range(HALVES):
+        wait_recv(post_slices[h].at[pl.ds(0, devices - 1)], 18 + h)
+
+        def pick(l):
+            for s in range(REMOTE):
+                parent = jnp.maximum(far_parent[l * REMOTE + s], 0)
+                post_send[h, l, s] = post_slices[h][parent]
+
+        def send_pick(l):
+            pick(l)
+            send(
+                post_send.at[h, l],
+                post_far.at[:, landing, lanes(h)],
+                22 + h,
+                l,
+                part,
+            )
+
+        each_leaf(send_pick)
+        pick(leaf)
+        post_far[:, landing, lanes(h)] = post_send[h, leaf]
+
+    def update_of(c, found):
+        share = (found / linear_low[c]).astype(jnp.bfloat16)
+        return finished(share, scaled_low[c], trans_low[c, quarter_of(part), :])
+
+    for h in range(HALVES):
+        wait_recv(post_mid.at[h, pl.ds(0, states - share_rows)], 20 + h)
+
+    def near_update(c, carry):
+        update_low[c] = update_of(c, post_near[jnp.minimum(place[c], mid_count - 1)])
+        return carry
+
+    lax.fori_loop(0, low_count, near_update, 0)
+    wait_recv(counts_mid.at[pl.ds(0, parts - 1)], 2)
+    update_mid[...] = counts_mid[...]
+    for h in range(HALVES):
+        wait_recv(post_send.at[h, pl.ds(0, leaves - 1)], 22 + h)
+
+    def far_update(s, carry):
+        far_counts[s] = update_of(far_index[s], post_far[s])
+        return carry
+
+    lax.fori_loop(0, REMOTE, far_update, 0)
+
+    def choose(c, carry):
+        slot = place[c] - mid_count
+        update_low[c] = jnp.where(
+            slot >= 0, far_counts[jnp.maximum(slot, 0)], update_low[c]
+        )
+        return carry
+
+    lax.fori_loop(0, low_count, choose, 0)
+
+    wait_send(pix.at[pl.ds(0, parts - 1)], 0)
+    wait_send(own_top.at[pl.ds(0, states - rows)], 1)
+    wait_send(counts_mid.at[pl.ds(0, parts - 1)], 2)
+    for h in range(HALVES):
+        wait_send(far_slices.at[h, pl.ds(0, leaves - 1)], 10 + h)
+        wait_send(mid_send.at[h, pl.ds(0, devices - 1)], 12 + h)
+        wait_send(up_slices.at[h, pl.ds(0, devices - 1)], 14 + h)
+        wait_send(total_send.at[h, pl.ds(0, devices - 1)], 16 + h)
+        wait_send(post_slices[h].at[pl.ds(0, devices - 1)], 18 + h)
+        wait_send(post_mid.at[h, pl.ds(0, states - share_rows)], 20 + h)
+        wait_send(post_send.at[h, pl.ds(0, leaves - 1)], 22 + h)
+
+
+def fused(
+    leaves,
+    parts,
+    pixels_low,
+    pixels_mid,
+    pixels_top,
+    emit_low,
+    emit_mid,
+    emit_top,
+    trans_low,
+    trans_mid,
+    outside_top,
+    parent_low,
+    parent_mid,
+):
+    low_count, images = pixels_low.shape
+    mid_count = pixels_mid.shape[0]
+    states = trans_low.shape[2]
+    devices = leaves * parts
+    share_rows = states // parts
+    rows = states // devices
+    whole = images * parts
+    wide = whole // HALVES
+    held = -(-(low_count + mid_count) // 8) * 8
+    real, half = jnp.float32, jnp.bfloat16
+    vmem = pltpu.VMEM
+    arrays = (pixels_low, pixels_mid, pixels_top, emit_low, emit_mid, emit_top, trans_low)
+    arrays += (trans_mid, outside_top)
+    return pl.pallas_call(
+        functools.partial(kernel, leaves, parts),
+        out_shape=(
+            jax.ShapeDtypeStruct((low_count, share_rows, states), real),
+            jax.ShapeDtypeStruct((mid_count, share_rows, states), real),
+        ),
+        in_specs=[pl.BlockSpec(memory_space=pltpu.SMEM)] * 2
+        + [pl.BlockSpec(memory_space=pltpu.HBM)] * len(arrays),
+        out_specs=(pl.BlockSpec(memory_space=pltpu.VMEM),) * 2,
+        scratch_shapes=[
+            pltpu.SMEM((REMOTE,), jnp.int32),
+            pltpu.SMEM((leaves * REMOTE,), jnp.int32),
+            pltpu.SMEM((low_count,), jnp.int32),
+            vmem(pixels_low.shape, jnp.int32),
+            vmem(pixels_mid.shape, jnp.int32),
+            vmem(pixels_top.shape, jnp.int32),
+            vmem(emit_low.shape, half),
+            vmem(emit_mid.shape[1:], half),
+            vmem(emit_top.shape, half),
+            vmem(trans_low.shape, half),
+            vmem(trans_mid.shape[1:], half),
+            vmem(outside_top.shape, real),
+            vmem((parts, held, images), jnp.int32),
+            vmem((leaves, rows, whole), real),
+            vmem((states, images), real),
+            vmem((HALVES, REMOTE, states, wide), real),
+            vmem((HALVES, leaves, REMOTE, rows, wide), real),
+            vmem((HALVES, devices, rows, wide), real),
+            vmem((HALVES, states, wide), real),
+            vmem((states, whole), real),
+            vmem((low_count, states, whole), half),
+            vmem((low_count, share_rows, whole), real),
+            vmem((states, whole), real),
+            vmem((HALVES, states, wide), real),
+            vmem((HALVES, devices, rows, wide), real),
+            vmem((HALVES, leaves, rows, wide), real),
+            vmem((HALVES, devices, rows, wide), real),
+            vmem((HALVES, states, wide), real),
+            vmem((states, whole), half),
+            vmem((HALVES, states, wide), real),
+            vmem((states, whole), half),
+            vmem((HALVES, states, wide), real),
+            (vmem((devices, rows, wide), real),) * HALVES,
+            vmem((HALVES, leaves, REMOTE, rows, wide), real),
+            vmem((mid_count, share_rows, whole), real),
+            vmem((REMOTE, share_rows, whole), real),
+            vmem((mid_count, share_rows, states), real),
+            vmem((states, states), real),
+            vmem((REMOTE, share_rows, states), real),
+            pltpu.SemaphoreType.DMA((24,)),
+            pltpu.SemaphoreType.DMA((24,)),
+            pltpu.SemaphoreType.DMA((len(arrays),)),
+        ],
+        compiler_params=pltpu.CompilerParams(
+            collective_id=0, has_side_effects=True, vmem_limit_bytes=48 * 2**20
+        ),
+    )(parent_low, parent_mid, *arrays)
+
+
 def solution(mesh):
+    leaves, parts = mesh.shape["leaf"], mesh.shape["batch"]
+    fits = 256 % (8 * leaves * parts) == 0
+    chosen = functools.partial(fused, leaves, parts) if fits else body
     return jax.shard_map(
-        body,
+        chosen,
         mesh=mesh,
         in_specs=(
             P("leaf", "batch"),

time: 266 us -> 99.2 us (0.37)
  blocking collectives: 116 us -> 0 us
  Pallas kernels: 0 us -> 86.2 us
  waiting for transfers between devices: 79.4 us -> 0 us
  other arithmetic: 16.9 us -> 0 us
  between operations: 14.3 us -> 0.66 us
  matrix products: 11.7 us -> 0 us
  starting transfers between devices: 11.5 us -> 0 us
  local copies, waits for them, and re-layouts: 14.5 us -> 11.4 us
    all_to_all x5 -> x0, blocking collectives: 116 us -> none  [the longest x1 55.3 us: body(): lax.all_to_all(up_low, 'leaf', split_axis=1, concat_axis=0, tiled=True)]
    pallas_call x0 -> x1, Pallas kernels: none -> 86.2 us  [fused(): pl.pallas_call(functools.partial(kernel, leaves, parts), out_shape=(jax.S...]
    all_to_all x3 -> x0, waiting for transfers between devices: 47.6 us -> none  [the longest x1 27.7 us: body(): lax.all_to_all(spread_mid[parent_low], 'leaf', split_axis=0, concat_axis=...]
    reduce_scatter x2 -> x0, waiting for transfers between devices: 31.8 us -> none  [the longest x1 31.8 us: body(): lax.psum_scatter(counts_low, 'batch', scatter_dimension=1, tiled=True)]
    dot_general x8 -> x0, matrix products: 11.7 us -> none  [the longest x2 8.04 us: edge_all(): jnp.einsum('nbi,nbj->nij', share, scaled, preferred_element_type=jnp.floa...]
    all_to_all x3 -> x0, starting transfers between devices: 11.4 us -> none  [the longest x1 4.39 us: body(): lax.all_to_all(spread_mid[parent_low], 'leaf', split_axis=0, concat_axis=...]
    scatter-add x2 -> x0, other arithmetic: 11 us -> none  [the longest x1 7.56 us: body(): jax.ops.segment_sum(moved, parent_low, num_segments=mid_count * devices)]
    unnamed x31 -> x24, local copies, waits for them, and re-layouts: 3.9 us -> 11.4 us
  transfers between devices with their start and end apart: 5 -> 0, of which waited for: 4 -> 0; matrix products, arithmetic and copies ran while one was open for 5% -> 0% of each run, Pallas kernels for 0% -> 0%
where the time goes in v2:
time: 99.2 us; the launch traced here: 98.3 us
  Pallas kernels  86.2 us (87%)
  local copies, waits for them, and re-layouts  11.4 us (11%)
    pallas_call x1, Pallas kernels, fused(): pl.pallas_call(functools.partial(kernel, leaves, parts), out_shape=(jax.S...  86.2 us
    unnamed x24, local copies, waits for them, and re-layouts  11.4 us

profile of v2, /device:TPU:0, one launch (start us, length us, event | category | flops | bytes accessed | tf_op | source)
XLA Modules:
  0.0 98.3 jit_solution(13585006037277306401)
XLA Ops:
  0.6 0.0 copy-start
  0.6 1.3 %copy-done = bf16[10,256,256]{2,1,0:T(8,128)(2,1)S(1)} copy-done((bf16[10,256,256]{2,1,0:T(8,128)(2,1)S(1)}, bf16[10,256,256]{2,1,0:T(8,128)(2,1)}, u32[]{:S(2)}) %copy-start) | copy-done | bytes 1310744
  2.0 0.0 copy-start.1
  2.0 1.3 %copy-done.1 = bf16[10,256,256]{2,1,0:T(8,128)(2,1)S(1)} copy-done((bf16[10,256,256]{2,1,0:T(8,128)(2,1)S(1)}, bf16[10,256,256]{2,1,0:T(8,128)(2,1)}, u32[]{:S(2)}) %copy-start.1) | copy-done | bytes 1310744
  3.3 0.0 copy-start.2
  3.3 1.0 %copy-done.2 = bf16[4,256,256]{2,1,0:T(8,128)(2,1)S(1)} copy-done((bf16[4,256,256]{2,1,0:T(8,128)(2,1)S(1)}, bf16[4,256,256]{2,1,0:T(8,128)(2,1)}, u32[]{:S(2)}) %copy-start.2) | copy-done | bytes 524312
  4.3 0.0 copy-start.3
  4.3 1.0 %copy-done.3 = bf16[4,256,256]{2,1,0:T(8,128)(2,1)S(1)} copy-done((bf16[4,256,256]{2,1,0:T(8,128)(2,1)S(1)}, bf16[4,256,256]{2,1,0:T(8,128)(2,1)}, u32[]{:S(2)}) %copy-start.3) | copy-done | bytes 524312
  5.4 0.0 copy-start.4
  5.4 0.9 copy-done.4
  6.3 0.0 copy-start.5
  6.3 0.9 copy-done.5
  7.2 0.0 copy-start.6
  7.2 0.7 copy-done.6
  7.9 0.0 copy-start.7
  7.9 0.7 copy-done.7
  8.5 0.0 copy-start.8
  8.5 0.7 copy-done.8
  9.2 0.0 copy-start.9
  9.2 0.7 copy-done.9
  9.9 0.0 copy-start.10
  9.9 0.7 copy-done.10
  10.5 86.2 %shard_map.122 = (f32[10,64,256]{2,1,0:T(8,128)S(1)}, f32[4,64,256]{2,1,0:T(8,128)S(1)}) custom-call(s32[80]{0:T(128)S(1)} %copy-done.8, s32[32]{0:T(128)S(1)} %copy-done.9, s32[10,128]{1,0:T(8,128)S(1)} %copy-done.6, s32[4,128]{1,0:T(4,128)S(1)} %copy-done.7, s32[1,128]{1,0:T(1,128)S(1)} %copy-done.10, bf16[10,256,256]{2,1,0:T(8,128)(2,1)S(1)} %copy-done, ...), custom_call_target="tpu_custom_call" | custom-call | tf_op jit(solution)/shard_map/pallas_call | solution.py:519
  96.7 0.8 copy.15
  97.6 0.7 copy.16
Async XLA Ops:
  0.6 1.3 %copy-start = (bf16[10,256,256]{2,1,0:T(8,128)(2,1)S(1)}, bf16[10,256,256]{2,1,0:T(8,128)(2,1)}, u32[]{:S(2)}) copy-start(bf16[10,256,256]{2,1,0:T(8,128)(2,1)} %emit_low_hbm.1) | copy-start | bytes 3932164
  2.0 1.3 %copy-start.1 = (bf16[10,256,256]{2,1,0:T(8,128)(2,1)S(1)}, bf16[10,256,256]{2,1,0:T(8,128)(2,1)}, u32[]{:S(2)}) copy-start(bf16[10,256,256]{2,1,0:T(8,128)(2,1)} %trans_low_hbm.1) | copy-start | bytes 3932164
  3.3 1.0 %copy-start.2 = (bf16[4,256,256]{2,1,0:T(8,128)(2,1)S(1)}, bf16[4,256,256]{2,1,0:T(8,128)(2,1)}, u32[]{:S(2)}) copy-start(bf16[4,256,256]{2,1,0:T(8,128)(2,1)} %emit_mid_hbm.1) | copy-start | bytes 1572868
  4.3 1.0 %copy-start.3 = (bf16[4,256,256]{2,1,0:T(8,128)(2,1)S(1)}, bf16[4,256,256]{2,1,0:T(8,128)(2,1)}, u32[]{:S(2)}) copy-start(bf16[4,256,256]{2,1,0:T(8,128)(2,1)} %trans_mid_hbm.1) | copy-start | bytes 1572868
  5.4 0.9 copy-start.4
  6.3 0.9 copy-start.5
  7.2 0.7 copy-start.6
  7.9 0.7 copy-start.7
  8.5 0.7 copy-start.8
  9.2 0.7 copy-start.9
  9.9 0.7 copy-start.10

commit v3 on v2

--- a/solution.py
+++ b/solution.py
@@ -9,7 +9,7 @@
 
 PSEUDO = 0.001
 REMOTE = 3
-HALVES = 1
+HALVES = 2
 STRIDE = 13
 MESH = pl.DeviceIdType.MESH
 
@@ -570,7 +570,7 @@
             pltpu.SemaphoreType.DMA((len(arrays),)),
         ],
         compiler_params=pltpu.CompilerParams(
-            collective_id=0, has_side_effects=True, vmem_limit_bytes=48 * 2**20
+            collective_id=0, has_side_effects=True, vmem_limit_bytes=62 * 2**20
         ),
     )(parent_low, parent_mid, *arrays)
 

time: 99.2 us -> 82 us (0.83)
  local copies, waits for them, and re-layouts: 11.4 us -> 2.72 us
  Pallas kernels: 86.2 us -> 78.5 us
    unnamed x24 -> x4, local copies, waits for them, and re-layouts: 11.4 us -> 2.72 us
    pallas_call x1, Pallas kernels: 86.2 us -> 78.5 us  [fused(): pl.pallas_call(functools.partial(kernel, leaves, parts), out_shape=(jax.S...]
where the time goes in v3:
time: 82 us; the launch traced here: 81.8 us
  Pallas kernels  78.5 us (96%)
  local copies, waits for them, and re-layouts  2.72 us (3%)
    pallas_call x1, Pallas kernels, fused(): pl.pallas_call(functools.partial(kernel, leaves, parts), out_shape=(jax.S...  78.5 us
    unnamed x4, local copies, waits for them, and re-layouts  2.72 us

profile of v3, /device:TPU:0, one launch (start us, length us, event | category | flops | bytes accessed | tf_op | source)
XLA Modules:
  0.0 81.8 jit_solution(4197029341121742082)
XLA Ops:
  0.6 78.5 %shard_map.122 = (f32[10,64,256]{2,1,0:T(8,128)}, f32[4,64,256]{2,1,0:T(8,128)}) custom-call(s32[80]{0:T(128)} %parent_low.1, s32[32]{0:T(128)} %parent_mid.1, s32[10,128]{1,0:T(8,128)} %pixels_low_hbm.1, s32[4,128]{1,0:T(4,128)} %pixels_mid_hbm.1, s32[1,128]{1,0:T(1,128)} %pixels_top_hbm.1, bf16[10,256,256]{2,1,0:T(8,128)(2,1)} %emit_low_hbm.1, ...), custom_call_target="tpu_custom_call" | custom-call | tf_op jit(solution)/shard_map/pallas_call | solution.py:519
  79.1 0.0 copy-start
  79.1 2.0 %copy.15 = f32[10,64,256]{2,1,0:T(8,128)} copy(f32[10,64,256]{2,1,0:T(8,128)} %get-tuple-element.4) | data formatting | bytes 1310720
  81.1 0.0 copy-done
  81.1 0.7 copy.16
Async XLA Ops:
  79.1 2.0 %copy-start = (f32[4,64,256]{2,1,0:T(8,128)S(1)}, f32[4,64,256]{2,1,0:T(8,128)}, u32[]{:S(2)}) copy-start(f32[4,64,256]{2,1,0:T(8,128)} %get-tuple-element.5) | copy-start | bytes 786436

commit v4 on v3

--- a/solution.py
+++ b/solution.py
@@ -131,6 +131,8 @@
     linear_full,
     up_mid,
     up_slices,
+    partial_own,
+    partial_far,
     totals,
     total_send,
     total_mine,
@@ -166,12 +168,12 @@
         for i, (source, target) in enumerate(
             (
                 (pixels_low_hbm, pixels_low),
+                (emit_low_hbm, emit_low),
+                (trans_low_hbm, trans_low),
                 (pixels_mid_hbm, pixels_mid),
                 (pixels_top_hbm, pixels_top),
                 (emit_top_hbm, emit_top),
                 (outside_top_hbm, outside_top),
-                (emit_low_hbm, emit_low),
-                (trans_low_hbm, trans_low),
                 (emit_mid_hbm.at[part], emit_mid),
                 (trans_mid_hbm.at[part], trans_mid),
             )
@@ -185,6 +187,23 @@
 
     def quarter_of(q):
         return pl.ds(pl.multiple_of(q * share_rows, share_rows), share_rows)
+
+    side = leaves // 2
+    pairs = devices // 2
+    base = lax.div(leaf, side) * side
+    spot = lax.rem(me, pairs)
+
+    def tall_slice_of(l, q):
+        start = q * share_rows + lax.rem(l, side) * (2 * rows)
+        return pl.ds(pl.multiple_of(start, 2 * rows), 2 * rows)
+
+    def each_near(step):
+        def one(k, carry):
+            t = lax.rem(spot + 5 * k, pairs)
+            step(t, base + lax.div(t, parts), lax.rem(t, parts))
+            return carry
+
+        lax.fori_loop(1, pairs, one, 0)
 
     def lanes(h):
         return pl.ds(h * wide, wide)
@@ -267,62 +286,59 @@
     def picks(row):
         return jnp.where(levels == row, 1.0, 0.0).astype(jnp.bfloat16)
 
-    loads[0].wait()
-    loads[1].wait()
+    def scale(inside):
+        return jnp.exp(inside - jnp.max(inside, axis=0, keepdims=True))
+
+    for load in loads[0:3]:
+        load.wait()
+
+    def far(s, carry):
+        node = far_index[s]
+        inside = dot(emit_low[node], picks(pixels_low[pl.ds(node, 1), :]), 0, 0)
+        scaled = scale(inside).astype(jnp.bfloat16)
+        far_up[s] = jnp.log(dot(trans_low[node], scaled, 1, 0))
+        return carry
+
+    lax.fori_loop(0, REMOTE, far, 0)
+    mine = pl.ds(pl.multiple_of(part * images, images), images)
+    loads[3].wait()
     pix[part, 0:low_count, :] = pixels_low[...]
     pix[part, low_count : low_count + mid_count, :] = pixels_mid[...]
     pl.semaphore_wait(barrier, devices - 1)
     each_part(lambda q: send(pix.at[part], pix.at[part], 0, leaf, q))
-    for load in loads[2:5]:
+    each_other(
+        lambda t, l, q: send(
+            far_up.at[:, slice_of(l, q), :], far_slices.at[leaf, :, :, mine], 3, l, q
+        )
+    )
+    far_slices[leaf, :, :, mine] = far_up[:, slice_of(leaf, part), :]
+    for load in loads[4:7]:
         load.wait()
     own_top[...] = dot(emit_top[0], picks(pixels_top[...]), 0, 0) + outside_top[0].T
-    mine = pl.ds(pl.multiple_of(part * images, images), images)
-    each_other(
+    each_near(
         lambda t, l, q: send(
-            own_top.at[slice_of(l, q)], edge_top.at[leaf, :, mine], 1, l, q
+            own_top.at[tall_slice_of(l, q)],
+            edge_top.at[lax.rem(leaf, side), :, mine],
+            1,
+            l,
+            q,
         )
     )
-    edge_top[leaf, :, mine] = own_top[slice_of(leaf, part), :]
-    loads[5].wait()
-    loads[6].wait()
+    edge_top[lax.rem(leaf, side), :, mine] = own_top[tall_slice_of(leaf, part), :]
     wait_recv(pix.at[pl.ds(0, parts - 1)], 0)
 
-    def lookup(table, node, first, last):
+    def lookup(table, node):
         chosen = jnp.concatenate(
-            [picks(pix[q, pl.ds(node, 1), :]) for q in range(first, last)], axis=1
+            [picks(pix[q, pl.ds(node, 1), :]) for q in range(parts)], axis=1
         )
         return dot(table, chosen, 0, 0)
-
-    def scale(inside):
-        return jnp.exp(inside - jnp.max(inside, axis=0, keepdims=True))
-
-    per = parts // HALVES
-    for h in range(HALVES):
-
-        def far(s, carry):
-            node = far_index[s]
-            scaled = scale(lookup(emit_low[node], node, h * per, h * per + per))
-            far_up[h, s] = jnp.log(dot(trans_low[node], scaled.astype(jnp.bfloat16), 1, 0))
-            return carry
-
-        lax.fori_loop(0, REMOTE, far, 0)
-        each_leaf(
-            lambda l: send(
-                far_up.at[h, :, slice_of(l, part), :],
-                far_slices.at[h, leaf],
-                10 + h,
-                l,
-                part,
-            )
-        )
-        far_slices[h, leaf] = far_up[h, :, slice_of(leaf, part), :]
 
     loads[7].wait()
     loads[8].wait()
-    inside_own[...] = lookup(emit_mid[...], low_count + part, 0, parts)
+    inside_own[...] = lookup(emit_mid[...], low_count + part)
 
     def near(c, carry):
-        scaled = scale(lookup(emit_low[c], c, 0, parts)).astype(jnp.bfloat16)
+        scaled = scale(lookup(emit_low[c], c)).astype(jnp.bfloat16)
         scaled_low[c] = scaled
         linear = dot(trans_low[c], scaled, 1, 0)
         linear_full[...] = linear
@@ -333,15 +349,15 @@
 
     lax.fori_loop(0, low_count // 2, near, 0)
 
-    for h in range(HALVES):
-        wait_recv(far_slices.at[h, pl.ds(0, leaves - 1)], 10 + h)
+    wait_recv(far_up.at[:, pl.ds(0, states - rows)], 3)
+    for h in range(HALVES):
 
         def sum_far(t):
             total = jnp.zeros((rows, wide), jnp.float32)
             for l in range(leaves):
                 for s in range(REMOTE):
                     weight = jnp.where(far_parent[l * REMOTE + s] == t, 1.0, 0.0)
-                    total += weight * far_slices[h, l, s]
+                    total += weight * far_slices[l, s, :, lanes(h)]
             return total
 
         def send_sum(t, l, q):
@@ -362,36 +378,44 @@
         linear = dot(trans_mid[...], scaled, 1, 0)
         linear_mid[h] = linear
         up_mid[h] = jnp.log(linear)
-        each_other(
+        each_near(
             lambda t, l, q: send(
-                up_mid.at[h, slice_of(l, q)], up_slices.at[h, me], 14 + h, l, q
+                up_mid.at[h, tall_slice_of(l, q)], up_slices.at[h, spot], 14 + h, l, q
             )
         )
-        up_slices[h, me] = up_mid[h, slice_of(leaf, part), :]
-
-    wait_recv(own_top.at[pl.ds(0, states - rows)], 1)
-    for h in range(HALVES):
-        wait_recv(up_slices.at[h, pl.ds(0, devices - 1)], 14 + h)
+        up_slices[h, spot] = up_mid[h, tall_slice_of(leaf, part), :]
+
+    wait_recv(own_top.at[pl.ds(0, states - 2 * rows)], 1)
+    for h in range(HALVES):
+        wait_recv(up_slices.at[h, pl.ds(0, pairs - 1)], 14 + h)
 
         def top(r, carry):
-            total = edge_top[r, :, lanes(h)]
-            for p in range(devices):
-                weight = jnp.where(parent_mid[p] == r, 1.0, 0.0)
+            here = jnp.where(lax.div(r, side) == lax.div(leaf, side), 1.0, 0.0)
+            total = here * edge_top[lax.rem(r, side), :, lanes(h)]
+            for p in range(pairs):
+                weight = jnp.where(parent_mid[base * parts + p] == r, 1.0, 0.0)
                 total += weight * up_slices[h, p]
-            totals[h, r] = total
+            partial_own[h, r] = total
             return carry
 
         lax.fori_loop(0, leaves, top, 0)
+        send(partial_own.at[h], partial_far.at[h], 24 + h, lax.rem(leaf + side, leaves), part)
+
+    for h in range(HALVES):
+        wait_recv(partial_far.at[h], 24 + h)
+        totals[h] = partial_own[h] + partial_far[h]
 
         def send_total(t, l, q):
-            total_send[h, t] = totals[h, parent_mid[t]]
-            send(total_send.at[h, t], total_mine.at[h, slice_of(leaf, part)], 16 + h, l, q)
-
-        each_other(send_total)
-        total_mine[h, slice_of(leaf, part), :] = totals[h, parent_mid[me]]
-
-    for h in range(HALVES):
-        wait_recv(total_mine.at[h, pl.ds(0, states - rows)], 16 + h)
+            total_send[h, t] = totals[h, parent_mid[base * parts + t]]
+            send(
+                total_send.at[h, t], total_mine.at[h, tall_slice_of(leaf, part)], 16 + h, l, q
+            )
+
+        each_near(send_total)
+        total_mine[h, tall_slice_of(leaf, part), :] = totals[h, parent_mid[me]]
+
+    for h in range(HALVES):
+        wait_recv(total_mine.at[h, pl.ds(0, states - 2 * rows)], 16 + h)
         reached = scale(total_mine[h])
         share = (
             reached / (linear_mid[h] * jnp.sum(reached, axis=0, keepdims=True))
@@ -476,13 +500,14 @@
     lax.fori_loop(0, low_count, choose, 0)
 
     wait_send(pix.at[pl.ds(0, parts - 1)], 0)
-    wait_send(own_top.at[pl.ds(0, states - rows)], 1)
+    wait_send(own_top.at[pl.ds(0, states - 2 * rows)], 1)
     wait_send(counts_mid.at[pl.ds(0, parts - 1)], 2)
-    for h in range(HALVES):
-        wait_send(far_slices.at[h, pl.ds(0, leaves - 1)], 10 + h)
+    wait_send(far_up.at[:, pl.ds(0, states - rows)], 3)
+    for h in range(HALVES):
         wait_send(mid_send.at[h, pl.ds(0, devices - 1)], 12 + h)
-        wait_send(up_slices.at[h, pl.ds(0, devices - 1)], 14 + h)
-        wait_send(total_send.at[h, pl.ds(0, devices - 1)], 16 + h)
+        wait_send(up_slices.at[h, pl.ds(0, pairs - 1)], 14 + h)
+        wait_send(total_send.at[h, pl.ds(0, pairs - 1)], 16 + h)
+        wait_send(partial_own.at[h], 24 + h)
         wait_send(post_slices[h].at[pl.ds(0, devices - 1)], 18 + h)
         wait_send(post_mid.at[h, pl.ds(0, states - share_rows)], 20 + h)
         wait_send(post_send.at[h, pl.ds(0, leaves - 1)], 22 + h)
@@ -539,10 +564,10 @@
             vmem(trans_mid.shape[1:], half),
             vmem(outside_top.shape, real),
             vmem((parts, held, images), jnp.int32),
-            vmem((leaves, rows, whole), real),
+            vmem((leaves // 2, 2 * rows, whole), real),
             vmem((states, images), real),
-            vmem((HALVES, REMOTE, states, wide), real),
-            vmem((HALVES, leaves, REMOTE, rows, wide), real),
+            vmem((REMOTE, states, images), real),
+            vmem((leaves, REMOTE, rows, whole), real),
             vmem((HALVES, devices, rows, wide), real),
             vmem((HALVES, states, wide), real),
             vmem((states, whole), real),
@@ -550,9 +575,11 @@
             vmem((low_count, share_rows, whole), real),
             vmem((states, whole), real),
             vmem((HALVES, states, wide), real),
-            vmem((HALVES, devices, rows, wide), real),
-            vmem((HALVES, leaves, rows, wide), real),
-            vmem((HALVES, devices, rows, wide), real),
+            vmem((HALVES, devices // 2, 2 * rows, wide), real),
+            vmem((HALVES, leaves, 2 * rows, wide), real),
+            vmem((HALVES, leaves, 2 * rows, wide), real),
+            vmem((HALVES, leaves, 2 * rows, wide), real),
+            vmem((HALVES, devices // 2, 2 * rows, wide), real),
             vmem((HALVES, states, wide), real),
             vmem((states, whole), half),
             vmem((HALVES, states, wide), real),
@@ -565,8 +592,8 @@
             vmem((mid_count, share_rows, states), real),
             vmem((states, states), real),
             vmem((REMOTE, share_rows, states), real),
-            pltpu.SemaphoreType.DMA((24,)),
-            pltpu.SemaphoreType.DMA((24,)),
+            pltpu.SemaphoreType.DMA((26,)),
+            pltpu.SemaphoreType.DMA((26,)),
             pltpu.SemaphoreType.DMA((len(arrays),)),
         ],
         compiler_params=pltpu.CompilerParams(
@@ -577,7 +604,7 @@
 
 def solution(mesh):
     leaves, parts = mesh.shape["leaf"], mesh.shape["batch"]
-    fits = 256 % (8 * leaves * parts) == 0
+    fits = leaves % 2 == 0 and 256 % (8 * leaves * parts) == 0
     chosen = functools.partial(fused, leaves, parts) if fits else body
     return jax.shard_map(
         chosen,

time: 82 us -> 79.5 us (0.970)
  Pallas kernels: 78.5 us -> 75.9 us
    pallas_call x1, Pallas kernels: 78.5 us -> 75.9 us  [fused(): pl.pallas_call(functools.partial(kernel, leaves, parts), out_shape=(jax.S...]
where the time goes in v4:
time: 79.5 us; the launch traced here: 79.3 us
  Pallas kernels  75.9 us (95%)
  local copies, waits for them, and re-layouts  2.72 us (3%)
    pallas_call x1, Pallas kernels, fused(): pl.pallas_call(functools.partial(kernel, leaves, parts), out_shape=(jax.S...  75.9 us
    unnamed x4, local copies, waits for them, and re-layouts  2.72 us

profile of v4, /device:TPU:0, one launch (start us, length us, event | category | flops | bytes accessed | tf_op | source)
XLA Modules:
  0.0 79.3 jit_solution(6413924100105480639)
XLA Ops:
  0.6 75.9 %shard_map.122 = (f32[10,64,256]{2,1,0:T(8,128)}, f32[4,64,256]{2,1,0:T(8,128)}) custom-call(s32[80]{0:T(128)} %parent_low.1, s32[32]{0:T(128)} %parent_mid.1, s32[10,128]{1,0:T(8,128)} %pixels_low_hbm.1, s32[4,128]{1,0:T(4,128)} %pixels_mid_hbm.1, s32[1,128]{1,0:T(1,128)} %pixels_top_hbm.1, bf16[10,256,256]{2,1,0:T(8,128)(2,1)} %emit_low_hbm.1, ...), custom_call_target="tpu_custom_call" | custom-call | tf_op jit(solution)/shard_map/pallas_call | solution.py:544
  76.6 0.0 copy-start
  76.6 2.0 %copy.15 = f32[10,64,256]{2,1,0:T(8,128)} copy(f32[10,64,256]{2,1,0:T(8,128)} %get-tuple-element.4) | data formatting | bytes 1310720
  78.6 0.0 copy-done
  78.6 0.7 copy.16
Async XLA Ops:
  76.6 2.0 %copy-start = (f32[4,64,256]{2,1,0:T(8,128)S(1)}, f32[4,64,256]{2,1,0:T(8,128)}, u32[]{:S(2)}) copy-start(f32[4,64,256]{2,1,0:T(8,128)} %get-tuple-element.5) | copy-start | bytes 786436

commit v5 on v4

--- a/solution.py
+++ b/solution.py
@@ -128,7 +128,8 @@
     inside_own,
     scaled_low,
     linear_low,
-    linear_full,
+    near_sums,
+    inside_near,
     up_mid,
     up_slices,
     partial_own,
@@ -292,11 +293,13 @@
     for load in loads[0:3]:
         load.wait()
 
-    def far(s, carry):
-        node = far_index[s]
+    def message(node):
         inside = dot(emit_low[node], picks(pixels_low[pl.ds(node, 1), :]), 0, 0)
         scaled = scale(inside).astype(jnp.bfloat16)
-        far_up[s] = jnp.log(dot(trans_low[node], scaled, 1, 0))
+        return jnp.log(dot(trans_low[node], scaled, 1, 0))
+
+    def far(s, carry):
+        far_up[s] = message(far_index[s])
         return carry
 
     lax.fori_loop(0, REMOTE, far, 0)
@@ -325,6 +328,20 @@
         )
     )
     edge_top[lax.rem(leaf, side), :, mine] = own_top[tall_slice_of(leaf, part), :]
+
+    near_sums[...] = jnp.zeros(near_sums.shape, jnp.float32)
+
+    def near(c, carry):
+        up = message(c)
+        for m in range(mid_count):
+            parent = parent_low[leaf * low_count + c]
+            weight = jnp.where(parent == leaf * mid_count + m, 1.0, 0.0)
+            near_sums[m] += weight * up
+        return carry
+
+    lax.fori_loop(0, low_count, near, 0)
+    each_part(lambda q: send(near_sums.at[q], inside_near.at[:, mine], 4, leaf, q))
+    inside_near[:, mine] = near_sums[part]
     wait_recv(pix.at[pl.ds(0, parts - 1)], 0)
 
     def lookup(table, node):
@@ -337,41 +354,47 @@
     loads[8].wait()
     inside_own[...] = lookup(emit_mid[...], low_count + part)
 
-    def near(c, carry):
+    def whole(c, carry):
         scaled = scale(lookup(emit_low[c], c)).astype(jnp.bfloat16)
         scaled_low[c] = scaled
-        linear = dot(trans_low[c], scaled, 1, 0)
-        linear_full[...] = linear
-        linear_low[c] = linear_full[quarter_of(part), :]
-        weight = jnp.where(parent_low[leaf * low_count + c] == me, 1.0, 0.0)
-        inside_own[...] += weight * jnp.log(linear)
+        linear_low[c] = dot(trans_low[c, quarter_of(part), :], scaled, 1, 0)
         return carry
 
-    lax.fori_loop(0, low_count // 2, near, 0)
+    first, second = low_count * 3 // 5, low_count * 4 // 5
+    lax.fori_loop(0, first, whole, 0)
 
     wait_recv(far_up.at[:, pl.ds(0, states - rows)], 3)
-    for h in range(HALVES):
-
-        def sum_far(t):
-            total = jnp.zeros((rows, wide), jnp.float32)
-            for l in range(leaves):
-                for s in range(REMOTE):
-                    weight = jnp.where(far_parent[l * REMOTE + s] == t, 1.0, 0.0)
-                    total += weight * far_slices[l, s, :, lanes(h)]
-            return total
-
-        def send_sum(t, l, q):
-            mid_send[h, t] = sum_far(t)
-            send(mid_send.at[h, t], mid_sums.at[h, slice_of(leaf, part)], 12 + h, l, q)
-
-        each_other(send_sum)
-        mid_sums[h, slice_of(leaf, part), :] = sum_far(me)
-
-    lax.fori_loop(low_count // 2, low_count, near, 0)
+
+    def sum_far(t):
+        total = jnp.zeros((rows, images * parts), jnp.float32)
+        for l in range(leaves):
+            for s in range(REMOTE):
+                weight = jnp.where(far_parent[l * REMOTE + s] == t, 1.0, 0.0)
+                total += weight * far_slices[l, s]
+        return total
+
+    def send_half(h, t, l, q):
+        send(mid_send.at[h, t], mid_sums.at[h, slice_of(leaf, part)], 12 + h, l, q)
+
+    def send_sum(t, l, q):
+        total = sum_far(t)
+        for h in range(HALVES):
+            mid_send[h, t] = total[:, h * wide : (h + 1) * wide]
+        send_half(0, t, l, q)
+
+    each_other(send_sum)
+    for h in range(1, HALVES):
+        each_other(functools.partial(send_half, h))
+    total = sum_far(me)
+    for h in range(HALVES):
+        mid_sums[h, slice_of(leaf, part), :] = total[:, h * wide : (h + 1) * wide]
+
+    lax.fori_loop(first, second, whole, 0)
+    wait_recv(near_sums.at[pl.ds(0, parts - 1)], 4)
 
     for h in range(HALVES):
         wait_recv(mid_sums.at[h, pl.ds(0, states - rows)], 12 + h)
-        exact = scale(inside_own[:, lanes(h)] + mid_sums[h])
+        exact = scale(inside_own[:, lanes(h)] + inside_near[:, lanes(h)] + mid_sums[h])
         post_mid[h] = exact
         scaled = exact.astype(jnp.bfloat16)
         scaled_mid[:, lanes(h)] = scaled
@@ -444,6 +467,8 @@
     each_part(lambda q: send(counts_own.at[quarter_of(q)], counts_mid.at[part], 2, leaf, q))
     counts_mid[part] = counts_own[quarter_of(part), :]
 
+    lax.fori_loop(second, low_count, whole, 0)
+
     landing = pl.ds(pl.multiple_of(leaf * rows, rows), rows)
     for h in range(HALVES):
         wait_recv(post_slices[h].at[pl.ds(0, devices - 1)], 18 + h)
@@ -503,6 +528,7 @@
     wait_send(own_top.at[pl.ds(0, states - 2 * rows)], 1)
     wait_send(counts_mid.at[pl.ds(0, parts - 1)], 2)
     wait_send(far_up.at[:, pl.ds(0, states - rows)], 3)
+    wait_send(near_sums.at[pl.ds(0, parts - 1)], 4)
     for h in range(HALVES):
         wait_send(mid_send.at[h, pl.ds(0, devices - 1)], 12 + h)
         wait_send(up_slices.at[h, pl.ds(0, pairs - 1)], 14 + h)
@@ -573,6 +599,7 @@
             vmem((states, whole), real),
             vmem((low_count, states, whole), half),
             vmem((low_count, share_rows, whole), real),
+            vmem((mid_count, states, images), real),
             vmem((states, whole), real),
             vmem((HALVES, states, wide), real),
             vmem((HALVES, devices // 2, 2 * rows, wide), real),

time: 79.5 us -> 79.7 us (level)
  no operation moved by 1% of the time
where the time goes in v5:
time: 79.7 us; the launch traced here: 79.5 us
  Pallas kernels  76.2 us (96%)
  local copies, waits for them, and re-layouts  2.72 us (3%)
    pallas_call x1, Pallas kernels, fused(): pl.pallas_call(functools.partial(kernel, leaves, parts), out_shape=(jax.S...  76.2 us
    unnamed x4, local copies, waits for them, and re-layouts  2.72 us

profile of v5, /device:TPU:0, one launch (start us, length us, event | category | flops | bytes accessed | tf_op | source)
XLA Modules:
  0.0 79.5 jit_solution(196738004254832552)
XLA Ops:
  0.6 76.2 %shard_map.122 = (f32[10,64,256]{2,1,0:T(8,128)}, f32[4,64,256]{2,1,0:T(8,128)}) custom-call(s32[80]{0:T(128)} %parent_low.1, s32[32]{0:T(128)} %parent_mid.1, s32[10,128]{1,0:T(8,128)} %pixels_low_hbm.1, s32[4,128]{1,0:T(4,128)} %pixels_mid_hbm.1, s32[1,128]{1,0:T(1,128)} %pixels_top_hbm.1, bf16[10,256,256]{2,1,0:T(8,128)(2,1)} %emit_low_hbm.1, ...), custom_call_target="tpu_custom_call" | custom-call | tf_op jit(solution)/shard_map/pallas_call | solution.py:570
  76.8 0.0 copy-start
  76.8 2.0 %copy.15 = f32[10,64,256]{2,1,0:T(8,128)} copy(f32[10,64,256]{2,1,0:T(8,128)} %get-tuple-element.4) | data formatting | bytes 1310720
  78.8 0.0 copy-done
  78.8 0.7 copy.16
Async XLA Ops:
  76.8 2.0 %copy-start = (f32[4,64,256]{2,1,0:T(8,128)S(1)}, f32[4,64,256]{2,1,0:T(8,128)}, u32[]{:S(2)}) copy-start(f32[4,64,256]{2,1,0:T(8,128)} %get-tuple-element.5) | copy-start | bytes 786436

commit v6 on v5

--- a/solution.py
+++ b/solution.py
@@ -132,8 +132,6 @@
     inside_near,
     up_mid,
     up_slices,
-    partial_own,
-    partial_far,
     totals,
     total_send,
     total_mine,
@@ -189,23 +187,6 @@
     def quarter_of(q):
         return pl.ds(pl.multiple_of(q * share_rows, share_rows), share_rows)
 
-    side = leaves // 2
-    pairs = devices // 2
-    base = lax.div(leaf, side) * side
-    spot = lax.rem(me, pairs)
-
-    def tall_slice_of(l, q):
-        start = q * share_rows + lax.rem(l, side) * (2 * rows)
-        return pl.ds(pl.multiple_of(start, 2 * rows), 2 * rows)
-
-    def each_near(step):
-        def one(k, carry):
-            t = lax.rem(spot + 5 * k, pairs)
-            step(t, base + lax.div(t, parts), lax.rem(t, parts))
-            return carry
-
-        lax.fori_loop(1, pairs, one, 0)
-
     def lanes(h):
         return pl.ds(h * wide, wide)
 
@@ -318,16 +299,12 @@
     for load in loads[4:7]:
         load.wait()
     own_top[...] = dot(emit_top[0], picks(pixels_top[...]), 0, 0) + outside_top[0].T
-    each_near(
+    each_other(
         lambda t, l, q: send(
-            own_top.at[tall_slice_of(l, q)],
-            edge_top.at[lax.rem(leaf, side), :, mine],
-            1,
-            l,
-            q,
+            own_top.at[slice_of(l, q)], edge_top.at[leaf, :, mine], 1, l, q
         )
     )
-    edge_top[lax.rem(leaf, side), :, mine] = own_top[tall_slice_of(leaf, part), :]
+    edge_top[leaf, :, mine] = own_top[slice_of(leaf, part), :]
 
     near_sums[...] = jnp.zeros(near_sums.shape, jnp.float32)
 
@@ -401,44 +378,36 @@
         linear = dot(trans_mid[...], scaled, 1, 0)
         linear_mid[h] = linear
         up_mid[h] = jnp.log(linear)
-        each_near(
+        each_other(
             lambda t, l, q: send(
-                up_mid.at[h, tall_slice_of(l, q)], up_slices.at[h, spot], 14 + h, l, q
+                up_mid.at[h, slice_of(l, q)], up_slices.at[h, me], 14 + h, l, q
             )
         )
-        up_slices[h, spot] = up_mid[h, tall_slice_of(leaf, part), :]
-
-    wait_recv(own_top.at[pl.ds(0, states - 2 * rows)], 1)
-    for h in range(HALVES):
-        wait_recv(up_slices.at[h, pl.ds(0, pairs - 1)], 14 + h)
+        up_slices[h, me] = up_mid[h, slice_of(leaf, part), :]
+
+    wait_recv(own_top.at[pl.ds(0, states - rows)], 1)
+    for h in range(HALVES):
+        wait_recv(up_slices.at[h, pl.ds(0, devices - 1)], 14 + h)
 
         def top(r, carry):
-            here = jnp.where(lax.div(r, side) == lax.div(leaf, side), 1.0, 0.0)
-            total = here * edge_top[lax.rem(r, side), :, lanes(h)]
-            for p in range(pairs):
-                weight = jnp.where(parent_mid[base * parts + p] == r, 1.0, 0.0)
+            total = edge_top[r, :, lanes(h)]
+            for p in range(devices):
+                weight = jnp.where(parent_mid[p] == r, 1.0, 0.0)
                 total += weight * up_slices[h, p]
-            partial_own[h, r] = total
+            totals[h, r] = total
             return carry
 
         lax.fori_loop(0, leaves, top, 0)
-        send(partial_own.at[h], partial_far.at[h], 24 + h, lax.rem(leaf + side, leaves), part)
-
-    for h in range(HALVES):
-        wait_recv(partial_far.at[h], 24 + h)
-        totals[h] = partial_own[h] + partial_far[h]
 
         def send_total(t, l, q):
-            total_send[h, t] = totals[h, parent_mid[base * parts + t]]
-            send(
-                total_send.at[h, t], total_mine.at[h, tall_slice_of(leaf, part)], 16 + h, l, q
-            )
-
-        each_near(send_total)
-        total_mine[h, tall_slice_of(leaf, part), :] = totals[h, parent_mid[me]]
-
-    for h in range(HALVES):
-        wait_recv(total_mine.at[h, pl.ds(0, states - 2 * rows)], 16 + h)
+            total_send[h, t] = totals[h, parent_mid[t]]
+            send(total_send.at[h, t], total_mine.at[h, slice_of(leaf, part)], 16 + h, l, q)
+
+        each_other(send_total)
+        total_mine[h, slice_of(leaf, part), :] = totals[h, parent_mid[me]]
+
+    for h in range(HALVES):
+        wait_recv(total_mine.at[h, pl.ds(0, states - rows)], 16 + h)
         reached = scale(total_mine[h])
         share = (
             reached / (linear_mid[h] * jnp.sum(reached, axis=0, keepdims=True))
@@ -525,15 +494,14 @@
     lax.fori_loop(0, low_count, choose, 0)
 
     wait_send(pix.at[pl.ds(0, parts - 1)], 0)
-    wait_send(own_top.at[pl.ds(0, states - 2 * rows)], 1)
+    wait_send(own_top.at[pl.ds(0, states - rows)], 1)
     wait_send(counts_mid.at[pl.ds(0, parts - 1)], 2)
     wait_send(far_up.at[:, pl.ds(0, states - rows)], 3)
     wait_send(near_sums.at[pl.ds(0, parts - 1)], 4)
     for h in range(HALVES):
         wait_send(mid_send.at[h, pl.ds(0, devices - 1)], 12 + h)
-        wait_send(up_slices.at[h, pl.ds(0, pairs - 1)], 14 + h)
-        wait_send(total_send.at[h, pl.ds(0, pairs - 1)], 16 + h)
-        wait_send(partial_own.at[h], 24 + h)
+        wait_send(up_slices.at[h, pl.ds(0, devices - 1)], 14 + h)
+        wait_send(total_send.at[h, pl.ds(0, devices - 1)], 16 + h)
         wait_send(post_slices[h].at[pl.ds(0, devices - 1)], 18 + h)
         wait_send(post_mid.at[h, pl.ds(0, states - share_rows)], 20 + h)
         wait_send(post_send.at[h, pl.ds(0, leaves - 1)], 22 + h)
@@ -570,8 +538,8 @@
     return pl.pallas_call(
         functools.partial(kernel, leaves, parts),
         out_shape=(
-            jax.ShapeDtypeStruct((low_count, share_rows, states), real),
-            jax.ShapeDtypeStruct((mid_count, share_rows, states), real),
+            vmem((low_count, share_rows, states), real),
+            vmem((mid_count, share_rows, states), real),
         ),
         in_specs=[pl.BlockSpec(memory_space=pltpu.SMEM)] * 2
         + [pl.BlockSpec(memory_space=pltpu.HBM)] * len(arrays),
@@ -590,7 +558,7 @@
             vmem(trans_mid.shape[1:], half),
             vmem(outside_top.shape, real),
             vmem((parts, held, images), jnp.int32),
-            vmem((leaves // 2, 2 * rows, whole), real),
+            vmem((leaves, rows, whole), real),
             vmem((states, images), real),
             vmem((REMOTE, states, images), real),
             vmem((leaves, REMOTE, rows, whole), real),
@@ -602,11 +570,9 @@
             vmem((mid_count, states, images), real),
             vmem((states, whole), real),
             vmem((HALVES, states, wide), real),
-            vmem((HALVES, devices // 2, 2 * rows, wide), real),
-            vmem((HALVES, leaves, 2 * rows, wide), real),
-            vmem((HALVES, leaves, 2 * rows, wide), real),
-            vmem((HALVES, leaves, 2 * rows, wide), real),
-            vmem((HALVES, devices // 2, 2 * rows, wide), real),
+            vmem((HALVES, devices, rows, wide), real),
+            vmem((HALVES, leaves, rows, wide), real),
+            vmem((HALVES, devices, rows, wide), real),
             vmem((HALVES, states, wide), real),
             vmem((states, whole), half),
             vmem((HALVES, states, wide), real),
@@ -619,8 +585,8 @@
             vmem((mid_count, share_rows, states), real),
             vmem((states, states), real),
             vmem((REMOTE, share_rows, states), real),
-            pltpu.SemaphoreType.DMA((26,)),
-            pltpu.SemaphoreType.DMA((26,)),
+            pltpu.SemaphoreType.DMA((24,)),
+            pltpu.SemaphoreType.DMA((24,)),
             pltpu.SemaphoreType.DMA((len(arrays),)),
         ],
         compiler_params=pltpu.CompilerParams(
@@ -631,7 +597,7 @@
 
 def solution(mesh):
     leaves, parts = mesh.shape["leaf"], mesh.shape["batch"]
-    fits = leaves % 2 == 0 and 256 % (8 * leaves * parts) == 0
+    fits = 256 % (8 * leaves * parts) == 0
     chosen = functools.partial(fused, leaves, parts) if fits else body
     return jax.shard_map(
         chosen,

time: 79.7 us -> 78.5 us (0.985)
  local copies, waits for them, and re-layouts: 2.72 us -> 1.54 us
    unnamed x4 -> x2, local copies, waits for them, and re-layouts: 2.72 us -> 1.54 us
where the time goes in v6:
time: 78.5 us; the launch traced here: 78.3 us
  Pallas kernels  76.2 us (97%)
  local copies, waits for them, and re-layouts  1.54 us (2%)
    pallas_call x1, Pallas kernels, fused(): pl.pallas_call(functools.partial(kernel, leaves, parts), out_shape=(vmem(...  76.2 us

profile of v6, /device:TPU:0, one launch (start us, length us, event | category | flops | bytes accessed | tf_op | source)
XLA Modules:
  0.0 78.3 jit_solution(15377457081036739237)
XLA Ops:
  0.6 76.2 %shard_map.122 = (f32[10,64,256]{2,1,0:T(8,128)S(1)}, f32[4,64,256]{2,1,0:T(8,128)S(1)}) custom-call(s32[80]{0:T(128)} %parent_low.1, s32[32]{0:T(128)} %parent_mid.1, s32[10,128]{1,0:T(8,128)} %pixels_low_hbm.1, s32[4,128]{1,0:T(4,128)} %pixels_mid_hbm.1, s32[1,128]{1,0:T(1,128)} %pixels_top_hbm.1, bf16[10,256,256]{2,1,0:T(8,128)(2,1)} %emit_low_hbm.1, ...), custom_call_target="tpu_custom_call" | custom-call | tf_op jit(solution)/shard_map/pallas_call | solution.py:538
  76.8 0.8 %copy.15 = f32[10,64,256]{2,1,0:T(8,128)} copy(f32[10,64,256]{2,1,0:T(8,128)S(1)} %get-tuple-element.2) | data formatting | bytes 1310720
  77.6 0.7 copy.16

commit v7 on v6

--- a/solution.py
+++ b/solution.py
@@ -128,8 +128,7 @@
     inside_own,
     scaled_low,
     linear_low,
-    near_sums,
-    inside_near,
+    linear_full,
     up_mid,
     up_slices,
     totals,
@@ -305,20 +304,6 @@
         )
     )
     edge_top[leaf, :, mine] = own_top[slice_of(leaf, part), :]
-
-    near_sums[...] = jnp.zeros(near_sums.shape, jnp.float32)
-
-    def near(c, carry):
-        up = message(c)
-        for m in range(mid_count):
-            parent = parent_low[leaf * low_count + c]
-            weight = jnp.where(parent == leaf * mid_count + m, 1.0, 0.0)
-            near_sums[m] += weight * up
-        return carry
-
-    lax.fori_loop(0, low_count, near, 0)
-    each_part(lambda q: send(near_sums.at[q], inside_near.at[:, mine], 4, leaf, q))
-    inside_near[:, mine] = near_sums[part]
     wait_recv(pix.at[pl.ds(0, parts - 1)], 0)
 
     def lookup(table, node):
@@ -331,14 +316,18 @@
     loads[8].wait()
     inside_own[...] = lookup(emit_mid[...], low_count + part)
 
-    def whole(c, carry):
+    def near(c, carry):
         scaled = scale(lookup(emit_low[c], c)).astype(jnp.bfloat16)
         scaled_low[c] = scaled
-        linear_low[c] = dot(trans_low[c, quarter_of(part), :], scaled, 1, 0)
+        linear = dot(trans_low[c], scaled, 1, 0)
+        linear_full[...] = linear
+        linear_low[c] = linear_full[quarter_of(part), :]
+        weight = jnp.where(parent_low[leaf * low_count + c] == me, 1.0, 0.0)
+        inside_own[...] += weight * jnp.log(linear)
         return carry
 
-    first, second = low_count * 3 // 5, low_count * 4 // 5
-    lax.fori_loop(0, first, whole, 0)
+    first = low_count * 7 // 10
+    lax.fori_loop(0, first, near, 0)
 
     wait_recv(far_up.at[:, pl.ds(0, states - rows)], 3)
 
@@ -366,12 +355,11 @@
     for h in range(HALVES):
         mid_sums[h, slice_of(leaf, part), :] = total[:, h * wide : (h + 1) * wide]
 
-    lax.fori_loop(first, second, whole, 0)
-    wait_recv(near_sums.at[pl.ds(0, parts - 1)], 4)
+    lax.fori_loop(first, low_count, near, 0)
 
     for h in range(HALVES):
         wait_recv(mid_sums.at[h, pl.ds(0, states - rows)], 12 + h)
-        exact = scale(inside_own[:, lanes(h)] + inside_near[:, lanes(h)] + mid_sums[h])
+        exact = scale(inside_own[:, lanes(h)] + mid_sums[h])
         post_mid[h] = exact
         scaled = exact.astype(jnp.bfloat16)
         scaled_mid[:, lanes(h)] = scaled
@@ -421,6 +409,8 @@
             )
         )
         post_slices[h][me] = post_mid[h, slice_of(leaf, part), :]
+
+    for h in range(HALVES):
         each_part(
             lambda q: send(
                 post_mid.at[h, quarter_of(q)], post_near.at[part, :, lanes(h)], 20 + h, leaf, q
@@ -433,10 +423,6 @@
         return states * counts / jnp.sum(counts, axis=-1, keepdims=True)
 
     counts_own[...] = finished(share_mid[...], scaled_mid[...], trans_mid[...])
-    each_part(lambda q: send(counts_own.at[quarter_of(q)], counts_mid.at[part], 2, leaf, q))
-    counts_mid[part] = counts_own[quarter_of(part), :]
-
-    lax.fori_loop(second, low_count, whole, 0)
 
     landing = pl.ds(pl.multiple_of(leaf * rows, rows), rows)
     for h in range(HALVES):
@@ -461,6 +447,9 @@
         pick(leaf)
         post_far[:, landing, lanes(h)] = post_send[h, leaf]
 
+    each_part(lambda q: send(counts_own.at[quarter_of(q)], counts_mid.at[part], 2, leaf, q))
+    counts_mid[part] = counts_own[quarter_of(part), :]
+
     def update_of(c, found):
         share = (found / linear_low[c]).astype(jnp.bfloat16)
         return finished(share, scaled_low[c], trans_low[c, quarter_of(part), :])
@@ -497,7 +486,6 @@
     wait_send(own_top.at[pl.ds(0, states - rows)], 1)
     wait_send(counts_mid.at[pl.ds(0, parts - 1)], 2)
     wait_send(far_up.at[:, pl.ds(0, states - rows)], 3)
-    wait_send(near_sums.at[pl.ds(0, parts - 1)], 4)
     for h in range(HALVES):
         wait_send(mid_send.at[h, pl.ds(0, devices - 1)], 12 + h)
         wait_send(up_slices.at[h, pl.ds(0, devices - 1)], 14 + h)
@@ -567,7 +555,6 @@
             vmem((states, whole), real),
             vmem((low_count, states, whole), half),
             vmem((low_count, share_rows, whole), real),
-            vmem((mid_count, states, images), real),
             vmem((states, whole), real),
             vmem((HALVES, states, wide), real),
             vmem((HALVES, devices, rows, wide), real),

time: 78.5 us -> 78.5 us (level)
  no operation moved by 1% of the time
where the time goes in v7:
time: 78.5 us; the launch traced here: 78.3 us
  Pallas kernels  76.1 us (97%)
  local copies, waits for them, and re-layouts  1.54 us (2%)
    pallas_call x1, Pallas kernels, fused(): pl.pallas_call(functools.partial(kernel, leaves, parts), out_shape=(vmem(...  76.1 us

profile of v7, /device:TPU:0, one launch (start us, length us, event | category | flops | bytes accessed | tf_op | source)
XLA Modules:
  0.0 78.3 jit_solution(3318024942287257177)
XLA Ops:
  0.6 76.1 %shard_map.122 = (f32[10,64,256]{2,1,0:T(8,128)S(1)}, f32[4,64,256]{2,1,0:T(8,128)S(1)}) custom-call(s32[80]{0:T(128)} %parent_low.1, s32[32]{0:T(128)} %parent_mid.1, s32[10,128]{1,0:T(8,128)} %pixels_low_hbm.1, s32[4,128]{1,0:T(4,128)} %pixels_mid_hbm.1, s32[1,128]{1,0:T(1,128)} %pixels_top_hbm.1, bf16[10,256,256]{2,1,0:T(8,128)(2,1)} %emit_low_hbm.1, ...), custom_call_target="tpu_custom_call" | custom-call | tf_op jit(solution)/shard_map/pallas_call | solution.py:526
  76.8 0.8 %copy.15 = f32[10,64,256]{2,1,0:T(8,128)} copy(f32[10,64,256]{2,1,0:T(8,128)S(1)} %get-tuple-element.2) | data formatting | bytes 1310720
  77.6 0.7 copy.16

commit v8 on v5

--- a/solution.py
+++ b/solution.py
@@ -128,8 +128,7 @@
     inside_own,
     scaled_low,
     linear_low,
-    near_sums,
-    inside_near,
+    linear_full,
     up_mid,
     up_slices,
     partial_own,
@@ -328,20 +327,6 @@
         )
     )
     edge_top[lax.rem(leaf, side), :, mine] = own_top[tall_slice_of(leaf, part), :]
-
-    near_sums[...] = jnp.zeros(near_sums.shape, jnp.float32)
-
-    def near(c, carry):
-        up = message(c)
-        for m in range(mid_count):
-            parent = parent_low[leaf * low_count + c]
-            weight = jnp.where(parent == leaf * mid_count + m, 1.0, 0.0)
-            near_sums[m] += weight * up
-        return carry
-
-    lax.fori_loop(0, low_count, near, 0)
-    each_part(lambda q: send(near_sums.at[q], inside_near.at[:, mine], 4, leaf, q))
-    inside_near[:, mine] = near_sums[part]
     wait_recv(pix.at[pl.ds(0, parts - 1)], 0)
 
     def lookup(table, node):
@@ -354,14 +339,18 @@
     loads[8].wait()
     inside_own[...] = lookup(emit_mid[...], low_count + part)
 
-    def whole(c, carry):
+    def near(c, carry):
         scaled = scale(lookup(emit_low[c], c)).astype(jnp.bfloat16)
         scaled_low[c] = scaled
-        linear_low[c] = dot(trans_low[c, quarter_of(part), :], scaled, 1, 0)
+        linear = dot(trans_low[c], scaled, 1, 0)
+        linear_full[...] = linear
+        linear_low[c] = linear_full[quarter_of(part), :]
+        weight = jnp.where(parent_low[leaf * low_count + c] == me, 1.0, 0.0)
+        inside_own[...] += weight * jnp.log(linear)
         return carry
 
-    first, second = low_count * 3 // 5, low_count * 4 // 5
-    lax.fori_loop(0, first, whole, 0)
+    first = low_count * 7 // 10
+    lax.fori_loop(0, first, near, 0)
 
     wait_recv(far_up.at[:, pl.ds(0, states - rows)], 3)
 
@@ -389,12 +378,11 @@
     for h in range(HALVES):
         mid_sums[h, slice_of(leaf, part), :] = total[:, h * wide : (h + 1) * wide]
 
-    lax.fori_loop(first, second, whole, 0)
-    wait_recv(near_sums.at[pl.ds(0, parts - 1)], 4)
+    lax.fori_loop(first, low_count, near, 0)
 
     for h in range(HALVES):
         wait_recv(mid_sums.at[h, pl.ds(0, states - rows)], 12 + h)
-        exact = scale(inside_own[:, lanes(h)] + inside_near[:, lanes(h)] + mid_sums[h])
+        exact = scale(inside_own[:, lanes(h)] + mid_sums[h])
         post_mid[h] = exact
         scaled = exact.astype(jnp.bfloat16)
         scaled_mid[:, lanes(h)] = scaled
@@ -452,6 +440,8 @@
             )
         )
         post_slices[h][me] = post_mid[h, slice_of(leaf, part), :]
+
+    for h in range(HALVES):
         each_part(
             lambda q: send(
                 post_mid.at[h, quarter_of(q)], post_near.at[part, :, lanes(h)], 20 + h, leaf, q
@@ -464,10 +454,6 @@
         return states * counts / jnp.sum(counts, axis=-1, keepdims=True)
 
     counts_own[...] = finished(share_mid[...], scaled_mid[...], trans_mid[...])
-    each_part(lambda q: send(counts_own.at[quarter_of(q)], counts_mid.at[part], 2, leaf, q))
-    counts_mid[part] = counts_own[quarter_of(part), :]
-
-    lax.fori_loop(second, low_count, whole, 0)
 
     landing = pl.ds(pl.multiple_of(leaf * rows, rows), rows)
     for h in range(HALVES):
@@ -492,6 +478,9 @@
         pick(leaf)
         post_far[:, landing, lanes(h)] = post_send[h, leaf]
 
+    each_part(lambda q: send(counts_own.at[quarter_of(q)], counts_mid.at[part], 2, leaf, q))
+    counts_mid[part] = counts_own[quarter_of(part), :]
+
     def update_of(c, found):
         share = (found / linear_low[c]).astype(jnp.bfloat16)
         return finished(share, scaled_low[c], trans_low[c, quarter_of(part), :])
@@ -528,7 +517,6 @@
     wait_send(own_top.at[pl.ds(0, states - 2 * rows)], 1)
     wait_send(counts_mid.at[pl.ds(0, parts - 1)], 2)
     wait_send(far_up.at[:, pl.ds(0, states - rows)], 3)
-    wait_send(near_sums.at[pl.ds(0, parts - 1)], 4)
     for h in range(HALVES):
         wait_send(mid_send.at[h, pl.ds(0, devices - 1)], 12 + h)
         wait_send(up_slices.at[h, pl.ds(0, pairs - 1)], 14 + h)
@@ -570,8 +558,8 @@
     return pl.pallas_call(
         functools.partial(kernel, leaves, parts),
         out_shape=(
-            jax.ShapeDtypeStruct((low_count, share_rows, states), real),
-            jax.ShapeDtypeStruct((mid_count, share_rows, states), real),
+            vmem((low_count, share_rows, states), real),
+            vmem((mid_count, share_rows, states), real),
         ),
         in_specs=[pl.BlockSpec(memory_space=pltpu.SMEM)] * 2
         + [pl.BlockSpec(memory_space=pltpu.HBM)] * len(arrays),
@@ -599,7 +587,6 @@
             vmem((states, whole), real),
             vmem((low_count, states, whole), half),
             vmem((low_count, share_rows, whole), real),
-            vmem((mid_count, states, images), real),
             vmem((states, whole), real),
             vmem((HALVES, states, wide), real),
             vmem((HALVES, devices // 2, 2 * rows, wide), real),

time: 79.7 us -> 77.5 us (0.972)
  local copies, waits for them, and re-layouts: 2.72 us -> 1.54 us
  Pallas kernels: 76.2 us -> 75.2 us
    unnamed x4 -> x2, local copies, waits for them, and re-layouts: 2.72 us -> 1.54 us
    pallas_call x1, Pallas kernels: 76.2 us -> 75.2 us  [fused(): pl.pallas_call(functools.partial(kernel, leaves, parts), out_shape=(vmem(...]
where the time goes in v8:
time: 77.5 us; the launch traced here: 77.4 us
  Pallas kernels  75.2 us (97%)
  local copies, waits for them, and re-layouts  1.54 us (2%)
    pallas_call x1, Pallas kernels, fused(): pl.pallas_call(functools.partial(kernel, leaves, parts), out_shape=(vmem(...  75.2 us

profile of v8, /device:TPU:0, one launch (start us, length us, event | category | flops | bytes accessed | tf_op | source)
XLA Modules:
  0.0 77.4 jit_solution(17903898831141779299)
XLA Ops:
  0.6 75.2 %shard_map.122 = (f32[10,64,256]{2,1,0:T(8,128)S(1)}, f32[4,64,256]{2,1,0:T(8,128)S(1)}) custom-call(s32[80]{0:T(128)} %parent_low.1, s32[32]{0:T(128)} %parent_mid.1, s32[10,128]{1,0:T(8,128)} %pixels_low_hbm.1, s32[4,128]{1,0:T(4,128)} %pixels_mid_hbm.1, s32[1,128]{1,0:T(1,128)} %pixels_top_hbm.1, bf16[10,256,256]{2,1,0:T(8,128)(2,1)} %emit_low_hbm.1, ...), custom_call_target="tpu_custom_call" | custom-call | tf_op jit(solution)/shard_map/pallas_call | solution.py:558
  75.8 0.8 %copy.15 = f32[10,64,256]{2,1,0:T(8,128)} copy(f32[10,64,256]{2,1,0:T(8,128)S(1)} %get-tuple-element.2) | data formatting | bytes 1310720
  76.7 0.7 copy.16
